TPU v7x, 32 devices: a whole 2x2x4 slice. The times are simulated.
32 devices in a mesh: rep: 2 (over y), dp: 16 (over z, x, core).
Axes of the slice: x: 2, y: 2, z: 4, core: 2. Of those that a mesh axis runs over, the one named last changes fastest.
Arguments:
- images: bfloat16 [256, 2, 1280], P(('rep', 'dp')), may hold values from -6 to 6
- weight: bfloat16 [1280, 8192], P(None, 'dp'), may hold values from -0.3354102 to 0.3354102, as said below
Outputs:
- image_grad: float32 [256, 2, 1280], P(('rep', 'dp'))
- weight_grad: float32 [1280, 8192], P(None, 'dp')
Inputs may be any that keep to these rules, and one draw needn't show every extreme that they name: `weight`: a projection whose columns have different scales.
All inputs are finite; a program needn't handle non-finite values.
Results may differ from a plain program's by a relative error of at most 0.0021.
Values may be sent and summed in bfloat16 or wider, within the bound.
No kernel may reach another device: no remote copies, remote signals or barrier semaphores. Data moves between devices by JAX's collectives and lax.ppermute only.
A program may use at most 64 MiB of HBM per device.

v0:
```python
import functools

import jax
import jax.numpy as jnp
from jax import lax
from jax.experimental import pallas as pl
from jax.experimental.pallas import tpu as pltpu
from jax.sharding import PartitionSpec as P

invariance_weight = 25.0
variance_weight = 25.0
covariance_weight = 1.0
loss_scale = 8192.0
epsilon_var = 0.0001

F32 = jnp.float32
BF16 = jnp.bfloat16
VMEM = pl.BlockSpec(memory_space=pltpu.VMEM)
SMEM = pl.BlockSpec(memory_space=pltpu.SMEM)
CORE, ACROSS, QUAD = 1, 2, 4
EXTRA = 8


def swap(block, axis, bits):
    return lax.ppermute(block, axis, [(i, i ^ bits) for i in range(lax.axis_size(axis))])


def centre(z):
    return z - jnp.mean(z, axis=0, keepdims=True)


def nt_dot(a, b):
    return lax.dot_general(a, b, (((1,), (1,)), ((), ())), preferred_element_type=F32)


def half_masks(half, count):
    row = lax.broadcasted_iota(jnp.int32, (half, count), 0)
    lane = lax.broadcasted_iota(jnp.int32, (half, count), 1)
    return (lane < half) & (row < lane), row == lane, lane < half


def whole(near_ref, far_ref):
    return jnp.concatenate([near_ref[...], far_ref[...]], axis=0)


def pick(me_ref, images_ref):
    images = images_ref[...].astype(F32)
    return jnp.where(me_ref[0] % 2 == 1, images[:, 1, :], images[:, 0, :])


def pick_kernel(me_ref, images_ref, rows_ref):
    rows_ref[...] = pick(me_ref, images_ref)


def pair_kernel(me_ref, rows_ref, images_ref, both_ref):
    rows = pick(me_ref, images_ref)
    both_ref[...] = jnp.concatenate([rows_ref[...], rows], axis=0).astype(BF16)


def turn_kernel(wide_ref, turned_ref):
    turned_ref[...] = jnp.swapaxes(wide_ref[...], 0, 1)


def gram_kernel(own, me_ref, near_ref, far_ref, c_ref, packed_ref, sorted_ref):
    me = me_ref[0]
    count, width = c_ref.shape
    devices = count // own
    outer = devices // QUAD
    half = count // 2
    centred = centre(whole(near_ref, far_ref)).reshape(devices, own, width)
    for slot in range(devices):
        rel = (slot // 2 % outer) * QUAD + (slot // 2 // outer) * 2 + slot % 2
        sorted_ref[rel ^ me] = centred[slot]
    c = sorted_ref[...].reshape(count, width).astype(BF16)
    c_ref[...] = c
    gram = nt_dot(c, c)
    upper, diagonal, _ = half_masks(half, count)
    turned = pltpu.roll(gram[half:], half, 1)
    packed_ref[:half] = jnp.where(upper, turned, gram[:half])
    second = jnp.sum(jnp.where(diagonal, turned, 0.0), axis=0, keepdims=True)
    packed_ref[half:] = jnp.broadcast_to(second, (EXTRA, count))


def unpack(packed_ref):
    count = packed_ref.shape[1]
    half = count // 2
    upper, diagonal, left = half_masks(half, count)
    top = packed_ref[:half]
    second = packed_ref[half:half + 1]
    mirror = jnp.swapaxes(jnp.concatenate([top, jnp.zeros_like(top)], axis=0), 0, 1)
    first = jnp.where(upper, mirror[:half], top)
    last = jnp.where(diagonal, second, jnp.where(upper, top, mirror[:half]))
    last = jnp.where(left, mirror[half:], pltpu.roll(last, half, 1))
    return first, last


def base_kernel(scale, features, near_ref, far_ref, base_ref):
    count = base_ref.shape[0]
    coeff = scale * 4.0 * covariance_weight / (features * (count - 1))
    centred = centre(whole(near_ref, far_ref))
    variance = jnp.sum(centred * centred, axis=0, keepdims=True) / (count - 1)
    spread = jnp.sqrt(variance + epsilon_var)
    wide = centred.astype(BF16).astype(F32)
    diag_cov = jnp.sum(wide * wide, axis=0, keepdims=True) / (count - 1)
    var_coeff = jnp.where(
        spread < 1.0, -scale * variance_weight / (features * (count - 1)) / spread, 0.0
    )
    base_ref[...] = var_coeff * centred - coeff * diag_cov * wide


def grads_kernel(own, scale, features, me_ref, packed_ref, c_ref, near_ref, far_ref, other_ref,
                 base_ref, w_ref, grad_ref, send_ref, gram_ref):
    me = me_ref[0]
    count, width = c_ref.shape
    devices = count // own
    half = count // 2
    first, last = unpack(packed_ref)
    gram_ref[:devices // 2] = first.reshape(devices // 2, own, count)
    gram_ref[devices // 2:] = last.reshape(devices // 2, own, count)
    order = [
        high * QUAD + across + core
        for across in (0, ACROSS) for high in range(devices // QUAD) for core in (0, CORE)
    ]
    rest = jnp.concatenate([gram_ref[rel ^ me] for rel in order], axis=0)
    through = 0.0
    for _ in range(2):
        piece = rest.astype(BF16)
        rest = rest - piece.astype(F32)
        through = through + jnp.dot(piece, c_ref[...], preferred_element_type=F32)
    coeff = scale * 4.0 * covariance_weight / (features * (count - 1))
    other = other_ref[...].reshape(devices // 2, 2, own, width)
    other = jnp.concatenate([other[:, 1:], other[:, :1]], axis=1).reshape(count, width)
    gap = whole(near_ref, far_ref) - other
    inv_term = gap * (scale * 2.0 * invariance_weight / (count * features))
    grad = (inv_term + base_ref[...] + through * (coeff / (count - 1))).astype(BF16)
    grad_ref[...] = grad
    send_ref[...] = jnp.dot(grad[count // 2:], w_ref[...], preferred_element_type=F32).astype(BF16)


def join_kernel(me_ref, own_ref, other_ref, out_ref):
    second = me_ref[0] % 2 == 1
    own, other = own_ref[...], other_ref[...]
    out_ref[:, 0, :] = jnp.where(second, other, own)
    out_ref[:, 1, :] = jnp.where(second, own, other)


def weight_operands(rows_ref, rows_core_ref, grad_ref, grad_core_ref):
    block = grad_core_ref.shape[1]
    rows = jnp.concatenate([rows_ref[...], rows_core_ref[...]], axis=0)
    return rows, jnp.concatenate([grad_ref[:, :block], grad_core_ref[...]], axis=0)


def tn_dot(a, b):
    return lax.dot_general(a, b, (((0,), (0,)), ((), ())), preferred_element_type=F32)


def weight_kernel(*refs):
    part = tn_dot(*weight_operands(*refs[:4]))
    refs[-1][...] = part + refs[4][...] if len(refs) > 5 else part


def last_weight_kernel(*refs):
    *operand_refs, earlier_ref, out_ref, sum_ref, sems = refs
    rows, grads = weight_operands(*operand_refs)
    bands, height, _ = sum_ref.shape
    copies = []
    for i in range(bands):
        band = slice(i * height, (i + 1) * height)
        sum_ref[i] = tn_dot(rows[:, band], grads) + earlier_ref[band]
        copies.append(pltpu.make_async_copy(sum_ref.at[i], out_ref.at[pl.ds(i * height, height)], sems.at[i]))
        copies[-1].start()
    for copy in copies:
        copy.wait()


def call(kernel, out_shape, specs, scratch=(), place=VMEM):
    return pl.pallas_call(
        kernel,
        out_shape=out_shape,
        in_specs=specs,
        out_specs=jax.tree.map(lambda _: place, out_shape),
        scratch_shapes=list(scratch),
        compiler_params=pltpu.CompilerParams(vmem_limit_bytes=32 * 1024 * 1024),
    )


def shards(images, weight):
    groups = lax.axis_size("rep")
    owners = lax.axis_size("dp")
    own, views, depth = images.shape
    block = weight.shape[1]
    width = 2 * block
    features = block * owners
    count = own * owners
    half = count // 2
    lot = 2 * own
    outer = owners // QUAD
    scale = loss_scale / groups
    position = lax.axis_index("dp")
    me = position.reshape(1)
    struct = jax.ShapeDtypeStruct

    def over_rep(array):
        return [
            lax.ppermute(array, "rep", [(i, (i + shift) % groups) for i in range(groups)])
            for shift in range(1, groups)
        ]

    def matmul(rows, matrix):
        return jnp.dot(rows, matrix, preferred_element_type=F32)

    given = swap(images, "dp", CORE)
    mine = call(pick_kernel, struct((own, depth), F32), [SMEM, VMEM])(me, images)
    given, mine, sent = lax.optimization_barrier((given, mine, weight))
    weight_core = swap(sent, "dp", CORE)
    mine = call(pair_kernel, struct((lot, depth), BF16), [SMEM] + [VMEM] * 2)(me, mine, given)
    column = [swap(mine, "dp", high * QUAD) for high in range(1, outer)]
    wide = jnp.concatenate([weight, weight_core], axis=1)
    column, wide = lax.optimization_barrier((column[::-1], wide))
    column = column[::-1]
    column = lax.optimization_barrier(jnp.concatenate([mine] + column, axis=0))
    across = swap(column, "dp", ACROSS)
    near = matmul(column, wide)
    wide_t = call(turn_kernel, struct((width, depth), BF16), [VMEM])(wide)
    wide_t, sent = lax.optimization_barrier((wide_t, column))
    near_others = over_rep(sent)
    near, across = lax.optimization_barrier((near, across))
    far = matmul(across, wide)

    c, packed = call(
        functools.partial(gram_kernel, own),
        (struct((count, width), BF16), struct((half + EXTRA, count), F32)),
        [SMEM] + [VMEM] * 2,
        [pltpu.VMEM((owners, own, width), F32)],
    )(me, near, far)

    top = owners // 2
    along, beside, corner = (swap(packed, "dp", bits) for bits in (ACROSS, top, ACROSS | top))
    corner, beside, along, wide_t = lax.optimization_barrier((corner, beside, along, wide_t))
    along, near_others = lax.optimization_barrier((along, near_others))
    packed = (packed + along) + (beside + corner)
    packed, near_late, far_late, rows = lax.optimization_barrier(
        (packed, near, far, jnp.concatenate([column, across], axis=0))
    )
    rows_core = swap(rows, "dp", CORE)
    base = call(
        functools.partial(base_kernel, scale, features), struct((count, width), F32), [VMEM] * 2
    )(near_late, far_late)
    base, sent = lax.optimization_barrier((base, across))
    far_others = over_rep(sent)
    other = matmul(rows_core, wide)
    bit = QUAD
    while bit < top:
        received = swap(packed, "dp", bit)
        received, other, base = lax.optimization_barrier((received, other, base))
        packed = packed + received
        bit *= 2

    grad, send = call(
        functools.partial(grads_kernel, own, scale, features),
        (struct((count, width), BF16), struct((half, depth), BF16)),
        [SMEM] + [VMEM] * 7,
        [pltpu.VMEM((owners, own, count), F32)],
    )(me, packed, c, near, far, other, base, wide_t)

    def weight_part(*operands):
        return call(weight_kernel, struct((depth, block), F32), [VMEM] * len(operands))(*operands)

    received = swap(send, "dp", ACROSS)
    keep = matmul(grad[:half], wide_t)
    grad_core = swap(grad[:, block:], "dp", CORE)
    keep, grad = lax.optimization_barrier((keep, grad))
    grad = grad[:, :block]
    grad_others, grad_core_others = over_rep(grad), over_rep(grad_core)
    keep = keep + received.astype(F32)
    keep, far_others = lax.optimization_barrier((keep, far_others))
    rows_others = [jnp.concatenate(pair, axis=0) for pair in zip(near_others, far_others)]
    keep = keep.reshape(outer, lot, depth)
    received = [
        swap(keep[high].astype(BF16), "dp", high * QUAD) for high in range(outer - 1, 0, -1)
    ]
    grad, grad_others, grad_core_others = lax.optimization_barrier(
        (grad, grad_others, grad_core_others)
    )
    weight_grad = weight_part(rows, rows_core, grad, grad_core)
    height = min(depth, 256)
    for left, (theirs, theirs_grad) in enumerate(zip(rows_others, grad_others), 2 - groups):
        operands = [
            theirs, swap(theirs, "dp", CORE),
            theirs_grad, grad_core_others.pop(0), weight_grad,
        ]
        if left < 0:
            weight_grad = weight_part(*operands)
        else:
            weight_grad = call(
                last_weight_kernel, struct((depth, block), F32), [VMEM] * 5,
                [
                    pltpu.VMEM((depth // height, height, block), F32),
                    pltpu.SemaphoreType.DMA((depth // height,)),
                ],
                pl.BlockSpec(memory_space=pl.ANY),
            )(*operands)
    received, weight_grad = lax.optimization_barrier((received, weight_grad))
    total = keep[0]
    for array in received:
        total = total + array.astype(F32)
    view_other = swap(total[own:], "dp", CORE)
    image_grad = call(join_kernel, struct((own, views, depth), F32), [SMEM] + [VMEM] * 2)(
        me, total[:own], view_other
    )
    return (image_grad, weight_grad)


def solution(mesh):
    return jax.shard_map(
        shards,
        mesh=mesh,
        in_specs=(P(("rep", "dp"), None, None), P(None, "dp")),
        out_specs=(P(("rep", "dp"), None, None), P(None, "dp")),
        check_vma=False,
    )
```

profile of v0, /device:TPU:0, one launch (start us, length us, event | category | flops | bytes accessed | tf_op | source)
XLA Modules:
  0.0 47.2 jit_solution(5132178122611994414)
XLA Ops:
  1.1 0.8 %copy-done = bf16[8,2,1280]{2,1,0:T(2,128)(2,1)S(1)} copy-done((bf16[8,2,1280]{2,1,0:T(2,128)(2,1)S(1)}, bf16[8,2,1280]{2,1,0:T(2,128)(2,1)}, u32[]{:S(2)}) %copy-start) | copy-done | bytes 40984
  2.6 4.8 %collective-permute-start.1 = (bf16[16,1280]{1,0:T(8,128)(2,1)S(1)}, bf16[16,1280]{1,0:T(8,128)(2,1)S(1)}, u32[]{:S(2)}, u32[]{:S(2)}) collective-permute-start(bf16[16,1280]{1,0:T(8,128)(2,1)S(1)} %shard_map.42), channel_id=1, source_target_pairs={{0,12},{1,13},{2,14},{3,15},{4,8},{5,9},{6,10},{7,11},{8,4},{9,5},... | collective-permute-start | bytes 122888 | tf_op jit(solution)/shard_map/ppermute | solution.py:25
  7.4 0.6 %collective-permute-start.3 = (bf16[16,1280]{1,0:T(8,128)(2,1)S(1)}, bf16[16,1280]{1,0:T(8,128)(2,1)S(1)}, u32[]{:S(2)}, u32[]{:S(2)}) collective-permute-start(bf16[16,1280]{1,0:T(8,128)(2,1)S(1)} %shard_map.42), channel_id=1, source_target_pairs={{0,4},{1,5},{2,6},{3,7},{4,0},{5,1},{6,2},{7,3},{8,12},{9,13},{10,... | collective-permute-start | bytes 122888 | tf_op jit(solution)/shard_map/ppermute | solution.py:25
  8.1 1.7 %pad_maximum_fusion.wide_ref = bf16[1280,1024]{1,0:T(8,128)(2,1)S(1)} fusion(bf16[1280,512]{1,0:T(8,128)(2,1)S(1)} %collective-permute-done.4, bf16[1280,512]{1,0:T(8,128)(2,1)} %param.3), kind=kLoop, calls=%fused_computation | loop fusion | flops 5242880 | bytes 5242880 | tf_op jit(solution)/shard_map/concatenate | solution.py:218
  9.8 2.6 %collective-permute-done.2 = bf16[16,1280]{1,0:T(8,128)(2,1)S(1)} collective-permute-done((bf16[16,1280]{1,0:T(8,128)(2,1)S(1)}, bf16[16,1280]{1,0:T(8,128)(2,1)S(1)}, u32[]{:S(2)}, u32[]{:S(2)}) %collective-permute-start.2) | collective-permute-done | bytes 40992 | tf_op jit(solution)/shard_map/ppermute | solution.py:25
  12.4 1.6 %collective-permute-start.5 = (bf16[64,1280]{1,0:T(8,128)(2,1)S(1)}, bf16[64,1280]{1,0:T(8,128)(2,1)S(1)}, u32[]{:S(2)}, u32[]{:S(2)}) collective-permute-start(bf16[64,1280]{1,0:T(8,128)(2,1)S(1)} %pad_maximum_fusion.2), channel_id=1, source_target_pairs={{0,2},{1,3},{2,0},{3,1},{4,6},{5,7},{6,4},{7,5},{8,10},{9,11},{10,... | collective-permute-start | bytes 491528 | tf_op jit(solution)/shard_map/ppermute | solution.py:25
  13.9 0.7 %shard_map.44.w_ref = bf16[1024,1280]{1,0:T(8,128)(2,1)S(1)} custom-call(bf16[1280,1024]{1,0:T(8,128)(2,1)S(1)} %pad_maximum_fusion.wide_ref), custom_call_target="tpu_custom_call" | custom-call | tf_op jit(solution)/shard_map/pallas_call | solution.py:224
  14.6 1.6 %collective-permute-start.9 = (bf16[64,1280]{1,0:T(8,128)(2,1)S(1)}, bf16[64,1280]{1,0:T(8,128)(2,1)S(1)}, u32[]{:S(2)}, u32[]{:S(2)}) collective-permute-start(bf16[64,1280]{1,0:T(8,128)(2,1)S(1)} %pad_maximum_fusion.2), channel_id=1, source_target_pairs={{0,16},{16,0},{1,17},{17,1},{2,18},{18,2},{3,19},{19,3},{4,20},{20... | collective-permute-start | bytes 491528 | tf_op jit(solution)/shard_map/ppermute | solution.py:205
  16.2 0.6 %fusion.4.near_ref = f32[64,1024]{1,0:T(8,128)S(1)} fusion(bf16[64,1280]{1,0:T(8,128)(2,1)S(1)} %pad_maximum_fusion.2, bf16[1280,1024]{1,0:T(8,128)(2,1)S(1)} %pad_maximum_fusion.wide_ref), kind=kOutput, calls=%fused_computation.12 | convolution fusion | flops 167772160 | bytes 3047424 | tf_op jit(solution)/shard_map/dot_general | solution.py:210
  16.8 1.1 %collective-permute-done.5 = bf16[64,1280]{1,0:T(8,128)(2,1)S(1)} collective-permute-done((bf16[64,1280]{1,0:T(8,128)(2,1)S(1)}, bf16[64,1280]{1,0:T(8,128)(2,1)S(1)}, u32[]{:S(2)}, u32[]{:S(2)}) %collective-permute-start.5) | collective-permute-done | bytes 163872 | tf_op jit(solution)/shard_map/ppermute | solution.py:25
  17.9 0.6 %fusion.5.far_ref = f32[64,1024]{1,0:T(8,128)S(1)} fusion(bf16[64,1280]{1,0:T(8,128)(2,1)S(1)} %collective-permute-done.5, bf16[1280,1024]{1,0:T(8,128)(2,1)S(1)} %pad_maximum_fusion.wide_ref), kind=kOutput, calls=%fused_computation.13 | convolution fusion | flops 167772160 | bytes 3047424 | tf_op jit(solution)/shard_map/dot_general | solution.py:210
  18.9 2.9 %collective-permute-start.6 = (f32[72,128]{1,0:T(8,128)S(1)}, f32[72,128]{1,0:T(8,128)S(1)}, u32[]{:S(2)}, u32[]{:S(2)}) collective-permute-start(f32[72,128]{1,0:T(8,128)S(1)} %get-tuple-element.52), channel_id=1, source_target_pairs={{0,10},{1,11},{2,8},{3,9},{4,14},{5,15},{6,12},{7,13},{8,2},{9,3},... | collective-permute-start | bytes 110600 | tf_op jit(solution)/shard_map/ppermute | solution.py:25
  21.7 1.0 %collective-permute-start.7 = (f32[72,128]{1,0:T(8,128)S(1)}, f32[72,128]{1,0:T(8,128)S(1)}, u32[]{:S(2)}, u32[]{:S(2)}) collective-permute-start(f32[72,128]{1,0:T(8,128)S(1)} %get-tuple-element.52), channel_id=1, source_target_pairs={{0,8},{1,9},{2,10},{3,11},{4,12},{5,13},{6,14},{7,15},{8,0},{9,1},... | collective-permute-start | bytes 110600 | tf_op jit(solution)/shard_map/ppermute | solution.py:25
  22.8 0.5 %collective-permute-start.8 = (f32[72,128]{1,0:T(8,128)S(1)}, f32[72,128]{1,0:T(8,128)S(1)}, u32[]{:S(2)}, u32[]{:S(2)}) collective-permute-start(f32[72,128]{1,0:T(8,128)S(1)} %get-tuple-element.52), channel_id=1, source_target_pairs={{0,2},{1,3},{2,0},{3,1},{4,6},{5,7},{6,4},{7,5},{8,10},{9,11},{10,... | collective-permute-start | bytes 110600 | tf_op jit(solution)/shard_map/ppermute | solution.py:25
  23.3 2.0 %collective-permute-done.6 = f32[72,128]{1,0:T(8,128)S(1)} collective-permute-done((f32[72,128]{1,0:T(8,128)S(1)}, f32[72,128]{1,0:T(8,128)S(1)}, u32[]{:S(2)}, u32[]{:S(2)}) %collective-permute-start.6) | collective-permute-done | bytes 36896 | tf_op jit(solution)/shard_map/ppermute | solution.py:25
  25.3 1.3 %collective-permute-done.7 = f32[72,128]{1,0:T(8,128)S(1)} collective-permute-done((f32[72,128]{1,0:T(8,128)S(1)}, f32[72,128]{1,0:T(8,128)S(1)}, u32[]{:S(2)}, u32[]{:S(2)}) %collective-permute-start.7) | collective-permute-done | bytes 36896 | tf_op jit(solution)/shard_map/ppermute | solution.py:25
  26.8 0.9 %collective-permute-start.10 = (f32[72,128]{1,0:T(8,128)S(1)}, f32[72,128]{1,0:T(8,128)S(1)}, u32[]{:S(2)}, u32[]{:S(2)}) collective-permute-start(f32[72,128]{1,0:T(8,128)S(1)} %add_add_fusion), channel_id=1, source_target_pairs={{0,4},{1,5},{2,6},{3,7},{4,0},{5,1},{6,2},{7,3},{8,12},{9,13},{10,... | collective-permute-start | bytes 110600 | tf_op jit(solution)/shard_map/ppermute | solution.py:25
  28.0 1.6 %collective-permute-start.13 = (bf16[64,1280]{1,0:T(8,128)(2,1)S(1)}, bf16[64,1280]{1,0:T(8,128)(2,1)S(1)}, u32[]{:S(2)}, u32[]{:S(2)}) collective-permute-start(bf16[64,1280]{1,0:T(8,128)(2,1)S(1)} %collective-permute-done.5), channel_id=1, source_target_pairs={{0,16},{16,0},{1,17},{17,1},{2,18},{18,2},{3,19},{19,3},{4,20},{20... | collective-permute-start | bytes 491528 | tf_op jit(solution)/shard_map/ppermute | solution.py:205
  30.1 0.8 %collective-permute-done.10 = f32[72,128]{1,0:T(8,128)S(1)} collective-permute-done((f32[72,128]{1,0:T(8,128)S(1)}, f32[72,128]{1,0:T(8,128)S(1)}, u32[]{:S(2)}, u32[]{:S(2)}) %collective-permute-start.10) | collective-permute-done | bytes 36896 | tf_op jit(solution)/shard_map/ppermute | solution.py:25
  30.9 1.0 %shard_map.46 = (bf16[128,1024]{1,0:T(8,128)(2,1)S(1)}, bf16[64,1280]{1,0:T(8,128)(2,1)S(1)}) custom-call(s32[1]{0:T(128)} %bitcast.me_ref, f32[72,128]{1,0:T(8,128)S(1)} %add.27.packed_ref, bf16[128,1024]{1,0:T(8,128)(2,1)S(1)} %get-tuple-element.65.c_ref, f32[64,1024]{1,0:T(8,128)S(1)} %fusion.4.near_ref, f32[64,1024]{1,0:T(8,128)S(1)} %fusion.5.far_ref, ...), custom_call_target="tpu_custom_call" | custom-call | tf_op jit(solution)/shard_map/pallas_call | solution.py:259
  31.9 0.6 %collective-permute-start.12 = (bf16[64,1280]{1,0:T(8,128)(2,1)S(1)}, bf16[64,1280]{1,0:T(8,128)(2,1)S(1)}, u32[]{:S(2)}, u32[]{:S(2)}) collective-permute-start(bf16[64,1280]{1,0:T(8,128)(2,1)S(1)} %get-tuple-element.71), channel_id=1, source_target_pairs={{0,2},{1,3},{2,0},{3,1},{4,6},{5,7},{6,4},{7,5},{8,10},{9,11},{10,... | collective-permute-start | bytes 491528 | tf_op jit(solution)/shard_map/ppermute | solution.py:25
  32.6 0.6 %fusion = f32[64,1280]{1,0:T(8,128)S(1)} fusion(bf16[1024,1280]{1,0:T(8,128)(2,1)S(1)} %shard_map.44.w_ref, bf16[128,1024]{1,0:T(8,128)(2,1)S(1)} %get-tuple-element.76), kind=kOutput, calls=%fused_computation.4 | convolution fusion | flops 167772160 | bytes 3080192 | tf_op jit(solution)/shard_map/dot_general | solution.py:210
  33.2 1.6 %collective-permute-start.18 = (bf16[128,512]{1,0:T(8,128)(2,1)S(1)}, bf16[128,512]{1,0:T(8,128)(2,1)S(1)}, u32[]{:S(2)}, u32[]{:S(2)}) collective-permute-start(bf16[128,512]{1,0:T(8,128)(2,1)S(1)} %slice.39.refs_2_), channel_id=1, source_target_pairs={{0,16},{16,0},{1,17},{17,1},{2,18},{18,2},{3,19},{19,3},{4,20},{20... | collective-permute-start | bytes 393224 | tf_op jit(solution)/shard_map/ppermute | solution.py:205
  34.8 0.7 %collective-permute-start.20 = (bf16[128,512]{1,0:T(8,128)(2,1)S(1)}, bf16[128,512]{1,0:T(8,128)(2,1)S(1)}, u32[]{:S(2)}, u32[]{:S(2)}) collective-permute-start(bf16[128,512]{1,0:T(8,128)(2,1)S(1)} %collective-permute-done.19.refs_3_), channel_id=1, source_target_pairs={{0,16},{16,0},{1,17},{17,1},{2,18},{18,2},{3,19},{19,3},{4,20},{20... | collective-permute-start | bytes 393224 | tf_op jit(solution)/shard_map/ppermute | solution.py:205
  35.5 1.9 %collective-permute-done.12 = bf16[64,1280]{1,0:T(8,128)(2,1)S(1)} collective-permute-done((bf16[64,1280]{1,0:T(8,128)(2,1)S(1)}, bf16[64,1280]{1,0:T(8,128)(2,1)S(1)}, u32[]{:S(2)}, u32[]{:S(2)}) %collective-permute-start.12) | collective-permute-done | bytes 163872 | tf_op jit(solution)/shard_map/ppermute | solution.py:25
  37.6 2.4 %collective-permute-start.14 = (bf16[16,1280]{1,0:T(8,128)(2,1)S(1)}, bf16[16,1280]{1,0:T(8,128)(2,1)S(1)}, u32[]{:S(2)}, u32[]{:S(2)}) collective-permute-start(bf16[16,1280]{1,0:T(8,128)(2,1)S(1)} %get-tuple-element.86), channel_id=1, source_target_pairs={{0,12},{1,13},{2,14},{3,15},{4,8},{5,9},{6,10},{7,11},{8,4},{9,5},... | collective-permute-start | bytes 122888 | tf_op jit(solution)/shard_map/ppermute | solution.py:25
  40.1 1.9 %collective-permute-start.16 = (bf16[16,1280]{1,0:T(8,128)(2,1)S(1)}, bf16[16,1280]{1,0:T(8,128)(2,1)S(1)}, u32[]{:S(2)}, u32[]{:S(2)}) collective-permute-start(bf16[16,1280]{1,0:T(8,128)(2,1)S(1)} %get-tuple-element.84), channel_id=1, source_target_pairs={{0,4},{1,5},{2,6},{3,7},{4,0},{5,1},{6,2},{7,3},{8,12},{9,13},{10,... | collective-permute-start | bytes 122888 | tf_op jit(solution)/shard_map/ppermute | solution.py:25
  42.0 0.5 %shard_map.47.refs_4_ = f32[1280,512]{1,0:T(8,128)S(1)} custom-call(bf16[128,1280]{1,0:T(8,128)(2,1)S(1)} %pad_maximum_fusion.1.refs_0_, bf16[128,1280]{1,0:T(8,128)(2,1)S(1)} %collective-permute-done.11.refs_1_, bf16[128,512]{1,0:T(8,128)(2,1)S(1)} %slice.39.refs_2_, bf16[128,512]{1,0:T(8,128)(2,1)S(1)} %collective-permute-done.19.refs_3_), custom_call_target="tpu_custom_call" | custom-call | tf_op jit(solution)/shard_map/pallas_call | solution.py:267
  42.6 1.8 %shard_map.48 = f32[1280,512]{1,0:T(8,128)} custom-call(bf16[128,1280]{1,0:T(8,128)(2,1)S(1)} %constant_dynamic-update-slice_fusion.refs_0_, bf16[128,1280]{1,0:T(8,128)(2,1)S(1)} %collective-permute-done.17.refs_1_, bf16[128,512]{1,0:T(8,128)(2,1)S(1)} %collective-permute-done.18.refs_2_, bf16[128,512]{1,0:T(8,128)(2,1)S(1)} %collective-permute-done.20.refs_3_, ...), custom_call_target="tpu_custom_call" | custom-call | tf_op jit(solution)/shard_map/pallas_call | solution.py:295
  44.4 0.8 %collective-permute-done.15 = bf16[16,1280]{1,0:T(8,128)(2,1)S(1)} collective-permute-done((bf16[16,1280]{1,0:T(8,128)(2,1)S(1)}, bf16[16,1280]{1,0:T(8,128)(2,1)S(1)}, u32[]{:S(2)}, u32[]{:S(2)}) %collective-permute-start.15) | collective-permute-done | bytes 40992 | tf_op jit(solution)/shard_map/ppermute | solution.py:25
  45.3 1.2 %collective-permute-done.21.other_ref = f32[8,1280]{1,0:T(8,128)S(1)} collective-permute-done((f32[8,1280]{1,0:T(8,128)S(1)}, f32[8,1280]{1,0:T(8,128)S(1)}, u32[]{:S(2)}, u32[]{:S(2)}) %collective-permute-start.21) | collective-permute-done | bytes 40992 | tf_op jit(solution)/shard_map/ppermute | solution.py:25
  46.5 0.7 %shard_map.49 = f32[8,2,1280]{2,1,0:T(2,128)} custom-call(s32[1]{0:T(128)} %bitcast.me_ref, f32[8,1280]{1,0:T(8,128)S(1)} %get-tuple-element.88.own_ref, f32[8,1280]{1,0:T(8,128)S(1)} %collective-permute-done.21.other_ref), custom_call_target="tpu_custom_call" | custom-call | tf_op jit(solution)/shard_map/pallas_call | solution.py:308
  (41 shorter events, 3.1 us)
Async XLA Ops:
  0.6 1.6 %collective-permute-start = (bf16[8,2,1280]{2,1,0:T(2,128)(2,1)}, bf16[8,2,1280]{2,1,0:T(2,128)(2,1)S(1)}, u32[]{:S(2)}, u32[]{:S(2)}) collective-permute-start(bf16[8,2,1280]{2,1,0:T(2,128)(2,1)} %images_ref.1), channel_id=1, source_target_pairs={{0,1},{1,0},{2,3},{3,2},{4,5},{5,4},{6,7},{7,6},{8,9},{9,8},{10,11... | collective-permute-start | bytes 122888 | tf_op jit(solution)/shard_map/ppermute | solution.py:25
  1.1 0.8 %copy-start = (bf16[8,2,1280]{2,1,0:T(2,128)(2,1)S(1)}, bf16[8,2,1280]{2,1,0:T(2,128)(2,1)}, u32[]{:S(2)}) copy-start(bf16[8,2,1280]{2,1,0:T(2,128)(2,1)} %images_ref.1) | copy-start | bytes 122884
  2.2 5.9 %collective-permute-start.4 = (bf16[1280,512]{1,0:T(8,128)(2,1)}, bf16[1280,512]{1,0:T(8,128)(2,1)S(1)}, u32[]{:S(2)}, u32[]{:S(2)}) collective-permute-start(bf16[1280,512]{1,0:T(8,128)(2,1)} %param.3), channel_id=1, source_target_pairs={{0,1},{1,0},{2,3},{3,2},{4,5},{5,4},{6,7},{7,6},{8,9},{9,8},{10,11... | collective-permute-start | bytes 3932168 | tf_op jit(solution)/shard_map/ppermute | solution.py:25
  2.6 7.2 %collective-permute-start.1 = (bf16[16,1280]{1,0:T(8,128)(2,1)S(1)}, bf16[16,1280]{1,0:T(8,128)(2,1)S(1)}, u32[]{:S(2)}, u32[]{:S(2)}) collective-permute-start(bf16[16,1280]{1,0:T(8,128)(2,1)S(1)} %shard_map.42), channel_id=1, source_target_pairs={{0,12},{1,13},{2,14},{3,15},{4,8},{5,9},{6,10},{7,11},{8,4},{9,5},... | collective-permute-start | bytes 122888 | tf_op jit(solution)/shard_map/ppermute | solution.py:25
  7.4 4.9 %collective-permute-start.2 = (bf16[16,1280]{1,0:T(8,128)(2,1)S(1)}, bf16[16,1280]{1,0:T(8,128)(2,1)S(1)}, u32[]{:S(2)}, u32[]{:S(2)}) collective-permute-start(bf16[16,1280]{1,0:T(8,128)(2,1)S(1)} %shard_map.42), channel_id=1, source_target_pairs={{0,8},{1,9},{2,10},{3,11},{4,12},{5,13},{6,14},{7,15},{8,0},{9,1},... | collective-permute-start | bytes 122888 | tf_op jit(solution)/shard_map/ppermute | solution.py:25
  7.4 4.9 %collective-permute-start.3 = (bf16[16,1280]{1,0:T(8,128)(2,1)S(1)}, bf16[16,1280]{1,0:T(8,128)(2,1)S(1)}, u32[]{:S(2)}, u32[]{:S(2)}) collective-permute-start(bf16[16,1280]{1,0:T(8,128)(2,1)S(1)} %shard_map.42), channel_id=1, source_target_pairs={{0,4},{1,5},{2,6},{3,7},{4,0},{5,1},{6,2},{7,3},{8,12},{9,13},{10,... | collective-permute-start | bytes 122888 | tf_op jit(solution)/shard_map/ppermute | solution.py:25
  12.4 5.5 %collective-permute-start.5 = (bf16[64,1280]{1,0:T(8,128)(2,1)S(1)}, bf16[64,1280]{1,0:T(8,128)(2,1)S(1)}, u32[]{:S(2)}, u32[]{:S(2)}) collective-permute-start(bf16[64,1280]{1,0:T(8,128)(2,1)S(1)} %pad_maximum_fusion.2), channel_id=1, source_target_pairs={{0,2},{1,3},{2,0},{3,1},{4,6},{5,7},{6,4},{7,5},{8,10},{9,11},{10,... | collective-permute-start | bytes 491528 | tf_op jit(solution)/shard_map/ppermute | solution.py:25
  14.6 12.1 %collective-permute-start.9 = (bf16[64,1280]{1,0:T(8,128)(2,1)S(1)}, bf16[64,1280]{1,0:T(8,128)(2,1)S(1)}, u32[]{:S(2)}, u32[]{:S(2)}) collective-permute-start(bf16[64,1280]{1,0:T(8,128)(2,1)S(1)} %pad_maximum_fusion.2), channel_id=1, source_target_pairs={{0,16},{16,0},{1,17},{17,1},{2,18},{18,2},{3,19},{19,3},{4,20},{20... | collective-permute-start | bytes 491528 | tf_op jit(solution)/shard_map/ppermute | solution.py:205
  18.9 6.4 %collective-permute-start.6 = (f32[72,128]{1,0:T(8,128)S(1)}, f32[72,128]{1,0:T(8,128)S(1)}, u32[]{:S(2)}, u32[]{:S(2)}) collective-permute-start(f32[72,128]{1,0:T(8,128)S(1)} %get-tuple-element.52), channel_id=1, source_target_pairs={{0,10},{1,11},{2,8},{3,9},{4,14},{5,15},{6,12},{7,13},{8,2},{9,3},... | collective-permute-start | bytes 110600 | tf_op jit(solution)/shard_map/ppermute | solution.py:25
  21.7 4.9 %collective-permute-start.7 = (f32[72,128]{1,0:T(8,128)S(1)}, f32[72,128]{1,0:T(8,128)S(1)}, u32[]{:S(2)}, u32[]{:S(2)}) collective-permute-start(f32[72,128]{1,0:T(8,128)S(1)} %get-tuple-element.52), channel_id=1, source_target_pairs={{0,8},{1,9},{2,10},{3,11},{4,12},{5,13},{6,14},{7,15},{8,0},{9,1},... | collective-permute-start | bytes 110600 | tf_op jit(solution)/shard_map/ppermute | solution.py:25
  22.8 4.0 %collective-permute-start.8 = (f32[72,128]{1,0:T(8,128)S(1)}, f32[72,128]{1,0:T(8,128)S(1)}, u32[]{:S(2)}, u32[]{:S(2)}) collective-permute-start(f32[72,128]{1,0:T(8,128)S(1)} %get-tuple-element.52), channel_id=1, source_target_pairs={{0,2},{1,3},{2,0},{3,1},{4,6},{5,7},{6,4},{7,5},{8,10},{9,11},{10,... | collective-permute-start | bytes 110600 | tf_op jit(solution)/shard_map/ppermute | solution.py:25
  26.7 2.8 %collective-permute-start.11 = (bf16[128,1280]{1,0:T(8,128)(2,1)S(1)}, bf16[128,1280]{1,0:T(8,128)(2,1)S(1)}, u32[]{:S(2)}, u32[]{:S(2)}) collective-permute-start(bf16[128,1280]{1,0:T(8,128)(2,1)S(1)} %pad_maximum_fusion.1.refs_0_), channel_id=1, source_target_pairs={{0,1},{1,0},{2,3},{3,2},{4,5},{5,4},{6,7},{7,6},{8,9},{9,8},{10,11... | collective-permute-start | bytes 983048 | tf_op jit(solution)/shard_map/ppermute | solution.py:25
  26.8 4.0 %collective-permute-start.10 = (f32[72,128]{1,0:T(8,128)S(1)}, f32[72,128]{1,0:T(8,128)S(1)}, u32[]{:S(2)}, u32[]{:S(2)}) collective-permute-start(f32[72,128]{1,0:T(8,128)S(1)} %add_add_fusion), channel_id=1, source_target_pairs={{0,4},{1,5},{2,6},{3,7},{4,0},{5,1},{6,2},{7,3},{8,12},{9,13},{10,... | collective-permute-start | bytes 110600 | tf_op jit(solution)/shard_map/ppermute | solution.py:25
  28.0 9.5 %collective-permute-start.13 = (bf16[64,1280]{1,0:T(8,128)(2,1)S(1)}, bf16[64,1280]{1,0:T(8,128)(2,1)S(1)}, u32[]{:S(2)}, u32[]{:S(2)}) collective-permute-start(bf16[64,1280]{1,0:T(8,128)(2,1)S(1)} %collective-permute-done.5), channel_id=1, source_target_pairs={{0,16},{16,0},{1,17},{17,1},{2,18},{18,2},{3,19},{19,3},{4,20},{20... | collective-permute-start | bytes 491528 | tf_op jit(solution)/shard_map/ppermute | solution.py:205
  31.9 5.5 %collective-permute-start.12 = (bf16[64,1280]{1,0:T(8,128)(2,1)S(1)}, bf16[64,1280]{1,0:T(8,128)(2,1)S(1)}, u32[]{:S(2)}, u32[]{:S(2)}) collective-permute-start(bf16[64,1280]{1,0:T(8,128)(2,1)S(1)} %get-tuple-element.71), channel_id=1, source_target_pairs={{0,2},{1,3},{2,0},{3,1},{4,6},{5,7},{6,4},{7,5},{8,10},{9,11},{10,... | collective-permute-start | bytes 491528 | tf_op jit(solution)/shard_map/ppermute | solution.py:25
  32.5 2.3 %collective-permute-start.19 = (bf16[128,512]{1,0:T(8,128)(2,1)S(1)}, bf16[128,512]{1,0:T(8,128)(2,1)S(1)}, u32[]{:S(2)}, u32[]{:S(2)}) collective-permute-start(bf16[128,512]{1,0:T(8,128)(2,1)S(1)} %slice.40), channel_id=1, source_target_pairs={{0,1},{1,0},{2,3},{3,2},{4,5},{5,4},{6,7},{7,6},{8,9},{9,8},{10,11... | collective-permute-start | bytes 393224 | tf_op jit(solution)/shard_map/ppermute | solution.py:25
  33.2 7.0 %collective-permute-start.18 = (bf16[128,512]{1,0:T(8,128)(2,1)S(1)}, bf16[128,512]{1,0:T(8,128)(2,1)S(1)}, u32[]{:S(2)}, u32[]{:S(2)}) collective-permute-start(bf16[128,512]{1,0:T(8,128)(2,1)S(1)} %slice.39.refs_2_), channel_id=1, source_target_pairs={{0,16},{16,0},{1,17},{17,1},{2,18},{18,2},{3,19},{19,3},{4,20},{20... | collective-permute-start | bytes 393224 | tf_op jit(solution)/shard_map/ppermute | solution.py:205
  34.8 7.2 %collective-permute-start.20 = (bf16[128,512]{1,0:T(8,128)(2,1)S(1)}, bf16[128,512]{1,0:T(8,128)(2,1)S(1)}, u32[]{:S(2)}, u32[]{:S(2)}) collective-permute-start(bf16[128,512]{1,0:T(8,128)(2,1)S(1)} %collective-permute-done.19.refs_3_), channel_id=1, source_target_pairs={{0,16},{16,0},{1,17},{17,1},{2,18},{18,2},{3,19},{19,3},{4,20},{20... | collective-permute-start | bytes 393224 | tf_op jit(solution)/shard_map/ppermute | solution.py:205
  37.5 5.1 %collective-permute-start.17 = (bf16[128,1280]{1,0:T(8,128)(2,1)S(1)}, bf16[128,1280]{1,0:T(8,128)(2,1)S(1)}, u32[]{:S(2)}, u32[]{:S(2)}) collective-permute-start(bf16[128,1280]{1,0:T(8,128)(2,1)S(1)} %constant_dynamic-update-slice_fusion.refs_0_), channel_id=1, source_target_pairs={{0,1},{1,0},{2,3},{3,2},{4,5},{5,4},{6,7},{7,6},{8,9},{9,8},{10,11... | collective-permute-start | bytes 983048 | tf_op jit(solution)/shard_map/ppermute | solution.py:25
  37.6 6.8 %collective-permute-start.14 = (bf16[16,1280]{1,0:T(8,128)(2,1)S(1)}, bf16[16,1280]{1,0:T(8,128)(2,1)S(1)}, u32[]{:S(2)}, u32[]{:S(2)}) collective-permute-start(bf16[16,1280]{1,0:T(8,128)(2,1)S(1)} %get-tuple-element.86), channel_id=1, source_target_pairs={{0,12},{1,13},{2,14},{3,15},{4,8},{5,9},{6,10},{7,11},{8,4},{9,5},... | collective-permute-start | bytes 122888 | tf_op jit(solution)/shard_map/ppermute | solution.py:25
  40.0 5.2 %collective-permute-start.15 = (bf16[16,1280]{1,0:T(8,128)(2,1)S(1)}, bf16[16,1280]{1,0:T(8,128)(2,1)S(1)}, u32[]{:S(2)}, u32[]{:S(2)}) collective-permute-start(bf16[16,1280]{1,0:T(8,128)(2,1)S(1)} %get-tuple-element.85), channel_id=1, source_target_pairs={{0,8},{1,9},{2,10},{3,11},{4,12},{5,13},{6,14},{7,15},{8,0},{9,1},... | collective-permute-start | bytes 122888 | tf_op jit(solution)/shard_map/ppermute | solution.py:25
  40.1 5.0 %collective-permute-start.16 = (bf16[16,1280]{1,0:T(8,128)(2,1)S(1)}, bf16[16,1280]{1,0:T(8,128)(2,1)S(1)}, u32[]{:S(2)}, u32[]{:S(2)}) collective-permute-start(bf16[16,1280]{1,0:T(8,128)(2,1)S(1)} %get-tuple-element.84), channel_id=1, source_target_pairs={{0,4},{1,5},{2,6},{3,7},{4,0},{5,1},{6,2},{7,3},{8,12},{9,13},{10,... | collective-permute-start | bytes 122888 | tf_op jit(solution)/shard_map/ppermute | solution.py:25
  45.2 1.3 %collective-permute-start.21 = (f32[8,1280]{1,0:T(8,128)S(1)}, f32[8,1280]{1,0:T(8,128)S(1)}, u32[]{:S(2)}, u32[]{:S(2)}) collective-permute-start(f32[8,1280]{1,0:T(8,128)S(1)} %get-tuple-element.87), channel_id=1, source_target_pairs={{0,1},{1,0},{2,3},{3,2},{4,5},{5,4},{6,7},{7,6},{8,9},{9,8},{10,11... | collective-permute-start | bytes 122888 | tf_op jit(solution)/shard_map/ppermute | solution.py:25
where the time goes:
time: 47.4 us; the launch traced here: 47.2 us
  starting transfers between devices  24 us (51%)
  waiting for transfers between devices  12 us (25%)
  Pallas kernels  5.43 us (11%)
  matrix products  2.23 us (5%)
  other arithmetic  1.8 us (4%)
  between operations  0.86 us (2%)
  local copies, waits for them, and re-layouts  0.84 us (2%)
    ppermute x18, starting transfers between devices, swap(): lax.ppermute(block, axis, [(i, i ^ bits) for i in range(lax.axis_size(axi...  18.6 us
    ppermute x18, waiting for transfers between devices, swap(): lax.ppermute(block, axis, [(i, i ^ bits) for i in range(lax.axis_size(axi...  12 us
    ppermute x4, starting transfers between devices, over_rep(): lax.ppermute(array, 'rep', [(i, (i + shift) % groups) for i in range(grou...  5.43 us
    dot_general x4, matrix products, matmul(): return jnp.dot(rows, matrix, preferred_element_type=F32)  2.23 us
    pallas_call x1, Pallas kernels, shards(): call(last_weight_kernel, struct((depth, block), F32), [VMEM] * 5, [pltpu....  1.79 us
    concatenate x1, other arithmetic, shards(): wide = jnp.concatenate([weight, weight_core], axis=1)  1.67 us
    pallas_call x1, Pallas kernels, shards(): call(functools.partial(grads_kernel, own, scale, features), (struct((coun...  1.04 us
  transfers between devices with their start and end apart: 22, of which 10 were waited for; matrix products, arithmetic and copies ran while one was open for 9% of the time, Pallas kernels for 10%

commit v1 on v0

--- a/solution.py
+++ b/solution.py
@@ -108,18 +108,18 @@
     base_ref[...] = var_coeff * centred - coeff * diag_cov * wide
 
 
-def grads_kernel(own, scale, features, me_ref, packed_ref, c_ref, near_ref, far_ref, other_ref,
-                 base_ref, w_ref, grad_ref, send_ref, gram_ref):
+def grads_kernel(side, scale, features, me_ref, packed_ref, c_ref, z_ref, other_ref, base_ref,
+                 w_ref, grad_ref, part_ref, gram_ref):
     me = me_ref[0]
-    count, width = c_ref.shape
-    devices = count // own
-    half = count // 2
+    count = c_ref.shape[0]
+    devices, own, _ = gram_ref.shape
+    half, width = z_ref.shape
     first, last = unpack(packed_ref)
     gram_ref[:devices // 2] = first.reshape(devices // 2, own, count)
     gram_ref[devices // 2:] = last.reshape(devices // 2, own, count)
     order = [
-        high * QUAD + across + core
-        for across in (0, ACROSS) for high in range(devices // QUAD) for core in (0, CORE)
+        high * QUAD + side * ACROSS + core
+        for high in range(devices // QUAD) for core in (0, CORE)
     ]
     rest = jnp.concatenate([gram_ref[rel ^ me] for rel in order], axis=0)
     through = 0.0
@@ -128,13 +128,14 @@
         rest = rest - piece.astype(F32)
         through = through + jnp.dot(piece, c_ref[...], preferred_element_type=F32)
     coeff = scale * 4.0 * covariance_weight / (features * (count - 1))
-    other = other_ref[...].reshape(devices // 2, 2, own, width)
-    other = jnp.concatenate([other[:, 1:], other[:, :1]], axis=1).reshape(count, width)
-    gap = whole(near_ref, far_ref) - other
-    inv_term = gap * (scale * 2.0 * invariance_weight / (count * features))
-    grad = (inv_term + base_ref[...] + through * (coeff / (count - 1))).astype(BF16)
+    rows = slice(side * half, (side + 1) * half)
+    other = other_ref[rows].reshape(half // (2 * own), 2, own, width)
+    other = jnp.concatenate([other[:, 1:], other[:, :1]], axis=1).reshape(half, width)
+    inv_term = (z_ref[...] - other) * (scale * 2.0 * invariance_weight / (count * features))
+    grad = (inv_term + base_ref[rows] + through * (coeff / (count - 1))).astype(BF16)
     grad_ref[...] = grad
-    send_ref[...] = jnp.dot(grad[count // 2:], w_ref[...], preferred_element_type=F32).astype(BF16)
+    part = jnp.dot(grad, w_ref[...], preferred_element_type=F32)
+    part_ref[...] = part.astype(part_ref.dtype)
 
 
 def join_kernel(me_ref, own_ref, other_ref, out_ref):
@@ -256,18 +257,23 @@
         packed = packed + received
         bit *= 2
 
-    grad, send = call(
-        functools.partial(grads_kernel, own, scale, features),
-        (struct((count, width), BF16), struct((half, depth), BF16)),
-        [SMEM] + [VMEM] * 7,
-        [pltpu.VMEM((owners, own, count), F32)],
-    )(me, packed, c, near, far, other, base, wide_t)
+    def grads(side, z, kind):
+        return call(
+            functools.partial(grads_kernel, side, scale, features),
+            (struct((half, width), BF16), struct((half, depth), kind)),
+            [SMEM] + [VMEM] * 6,
+            [pltpu.VMEM((owners, own, count), F32)],
+        )(me, packed, c, z, other, base, wide_t)
+
+    grad_far, send = grads(1, far, BF16)
 
     def weight_part(*operands):
         return call(weight_kernel, struct((depth, block), F32), [VMEM] * len(operands))(*operands)
 
     received = swap(send, "dp", ACROSS)
-    keep = matmul(grad[:half], wide_t)
+    _, late = lax.optimization_barrier((send, near))
+    grad_near, keep = grads(0, late, F32)
+    grad = jnp.concatenate([grad_near, grad_far], axis=0)
     grad_core = swap(grad[:, block:], "dp", CORE)
     keep, grad = lax.optimization_barrier((keep, grad))
     grad = grad[:, :block]

time: 47.4 us -> 47.1 us (level)
  waiting for transfers between devices: 12 us -> 11.2 us
  matrix products: 2.23 us -> 1.68 us
  Pallas kernels: 5.43 us -> 5.96 us
  starting transfers between devices: 24 us -> 24.5 us
    ppermute x18, waiting for transfers between devices: 12 us -> 11 us  [swap(): lax.ppermute(block, axis, [(i, i ^ bits) for i in range(lax.axis_size(axi...]
    ppermute x4, starting transfers between devices: 5.43 us -> 5.98 us  [over_rep(): lax.ppermute(array, 'rep', [(i, (i + shift) % groups) for i in range(grou...]
    dot_general x4 -> x3, matrix products: 2.23 us -> 1.68 us  [matmul(): return jnp.dot(rows, matrix, preferred_element_type=F32)]
    pallas_call x1 -> x2, Pallas kernels: 1.04 us -> 1.57 us  [grads(): call(functools.partial(grads_kernel, side, scale, features), (struct((hal...]
  transfers between devices with their start and end apart: 22 -> 22, of which waited for: 10 -> 11; matrix products, arithmetic and copies ran while one was open for 9% -> 7% of each run, Pallas kernels for 10% -> 11%
where the time goes in v1:
time: 47.1 us; the launch traced here: 46.9 us
  starting transfers between devices  24.5 us (52%)
  waiting for transfers between devices  11.2 us (24%)
  Pallas kernels  5.96 us (13%)
  other arithmetic  1.8 us (4%)
  matrix products  1.68 us (4%)
  between operations  0.88 us (2%)
  local copies, waits for them, and re-layouts  0.86 us (2%)
    ppermute x18, starting transfers between devices, swap(): lax.ppermute(block, axis, [(i, i ^ bits) for i in range(lax.axis_size(axi...  18.6 us
    ppermute x18, waiting for transfers between devices, swap(): lax.ppermute(block, axis, [(i, i ^ bits) for i in range(lax.axis_size(axi...  11 us
    ppermute x4, starting transfers between devices, over_rep(): lax.ppermute(array, 'rep', [(i, (i + shift) % groups) for i in range(grou...  5.98 us
    pallas_call x1, Pallas kernels, shards(): call(last_weight_kernel, struct((depth, block), F32), [VMEM] * 5, [pltpu....  1.79 us
    dot_general x3, matrix products, matmul(): return jnp.dot(rows, matrix, preferred_element_type=F32)  1.68 us
    concatenate x1, other arithmetic, shards(): wide = jnp.concatenate([weight, weight_core], axis=1)  1.67 us
    pallas_call x2, Pallas kernels, grads(): call(functools.partial(grads_kernel, side, scale, features), (struct((hal...  1.57 us
  transfers between devices with their start and end apart: 22, of which 11 were waited for; matrix products, arithmetic and copies ran while one was open for 7% of the time, Pallas kernels for 11%

profile of v1, /device:TPU:0, one launch (start us, length us, event | category | flops | bytes accessed | tf_op | source)
XLA Modules:
  0.0 46.9 jit_solution(4066071417789638602)
XLA Ops:
  1.1 0.8 %copy-done = bf16[8,2,1280]{2,1,0:T(2,128)(2,1)S(1)} copy-done((bf16[8,2,1280]{2,1,0:T(2,128)(2,1)S(1)}, bf16[8,2,1280]{2,1,0:T(2,128)(2,1)}, u32[]{:S(2)}) %copy-start) | copy-done | bytes 40984
  2.6 4.8 %collective-permute-start.1 = (bf16[16,1280]{1,0:T(8,128)(2,1)S(1)}, bf16[16,1280]{1,0:T(8,128)(2,1)S(1)}, u32[]{:S(2)}, u32[]{:S(2)}) collective-permute-start(bf16[16,1280]{1,0:T(8,128)(2,1)S(1)} %shard_map.42), channel_id=1, source_target_pairs={{0,12},{1,13},{2,14},{3,15},{4,8},{5,9},{6,10},{7,11},{8,4},{9,5},... | collective-permute-start | bytes 122888 | tf_op jit(solution)/shard_map/ppermute | solution.py:25
  7.4 0.6 %collective-permute-start.3 = (bf16[16,1280]{1,0:T(8,128)(2,1)S(1)}, bf16[16,1280]{1,0:T(8,128)(2,1)S(1)}, u32[]{:S(2)}, u32[]{:S(2)}) collective-permute-start(bf16[16,1280]{1,0:T(8,128)(2,1)S(1)} %shard_map.42), channel_id=1, source_target_pairs={{0,4},{1,5},{2,6},{3,7},{4,0},{5,1},{6,2},{7,3},{8,12},{9,13},{10,... | collective-permute-start | bytes 122888 | tf_op jit(solution)/shard_map/ppermute | solution.py:25
  8.1 1.7 %pad_maximum_fusion.wide_ref = bf16[1280,1024]{1,0:T(8,128)(2,1)S(1)} fusion(bf16[1280,512]{1,0:T(8,128)(2,1)S(1)} %collective-permute-done.4, bf16[1280,512]{1,0:T(8,128)(2,1)} %param.3), kind=kLoop, calls=%fused_computation | loop fusion | flops 5242880 | bytes 5242880 | tf_op jit(solution)/shard_map/concatenate | solution.py:219
  9.8 2.6 %collective-permute-done.2 = bf16[16,1280]{1,0:T(8,128)(2,1)S(1)} collective-permute-done((bf16[16,1280]{1,0:T(8,128)(2,1)S(1)}, bf16[16,1280]{1,0:T(8,128)(2,1)S(1)}, u32[]{:S(2)}, u32[]{:S(2)}) %collective-permute-start.2) | collective-permute-done | bytes 40992 | tf_op jit(solution)/shard_map/ppermute | solution.py:25
  12.4 1.6 %collective-permute-start.5 = (bf16[64,1280]{1,0:T(8,128)(2,1)S(1)}, bf16[64,1280]{1,0:T(8,128)(2,1)S(1)}, u32[]{:S(2)}, u32[]{:S(2)}) collective-permute-start(bf16[64,1280]{1,0:T(8,128)(2,1)S(1)} %pad_maximum_fusion.2), channel_id=1, source_target_pairs={{0,2},{1,3},{2,0},{3,1},{4,6},{5,7},{6,4},{7,5},{8,10},{9,11},{10,... | collective-permute-start | bytes 491528 | tf_op jit(solution)/shard_map/ppermute | solution.py:25
  13.9 0.7 %shard_map.44.w_ref = bf16[1024,1280]{1,0:T(8,128)(2,1)S(1)} custom-call(bf16[1280,1024]{1,0:T(8,128)(2,1)S(1)} %pad_maximum_fusion.wide_ref), custom_call_target="tpu_custom_call" | custom-call | tf_op jit(solution)/shard_map/pallas_call | solution.py:225
  14.6 1.6 %collective-permute-start.9 = (bf16[64,1280]{1,0:T(8,128)(2,1)S(1)}, bf16[64,1280]{1,0:T(8,128)(2,1)S(1)}, u32[]{:S(2)}, u32[]{:S(2)}) collective-permute-start(bf16[64,1280]{1,0:T(8,128)(2,1)S(1)} %pad_maximum_fusion.2), channel_id=1, source_target_pairs={{0,16},{16,0},{1,17},{17,1},{2,18},{18,2},{3,19},{19,3},{4,20},{20... | collective-permute-start | bytes 491528 | tf_op jit(solution)/shard_map/ppermute | solution.py:206
  16.2 0.6 %fusion.2.near_ref.z_ref = f32[64,1024]{1,0:T(8,128)S(1)} fusion(bf16[64,1280]{1,0:T(8,128)(2,1)S(1)} %pad_maximum_fusion.2, bf16[1280,1024]{1,0:T(8,128)(2,1)S(1)} %pad_maximum_fusion.wide_ref), kind=kOutput, calls=%fused_computation.12 | convolution fusion | flops 167772160 | bytes 3047424 | tf_op jit(solution)/shard_map/dot_general | solution.py:211
  16.8 1.1 %collective-permute-done.5 = bf16[64,1280]{1,0:T(8,128)(2,1)S(1)} collective-permute-done((bf16[64,1280]{1,0:T(8,128)(2,1)S(1)}, bf16[64,1280]{1,0:T(8,128)(2,1)S(1)}, u32[]{:S(2)}, u32[]{:S(2)}) %collective-permute-start.5) | collective-permute-done | bytes 163872 | tf_op jit(solution)/shard_map/ppermute | solution.py:25
  17.9 0.6 %fusion.3.far_ref.z_ref = f32[64,1024]{1,0:T(8,128)S(1)} fusion(bf16[64,1280]{1,0:T(8,128)(2,1)S(1)} %collective-permute-done.5, bf16[1280,1024]{1,0:T(8,128)(2,1)S(1)} %pad_maximum_fusion.wide_ref), kind=kOutput, calls=%fused_computation.13 | convolution fusion | flops 167772160 | bytes 3047424 | tf_op jit(solution)/shard_map/dot_general | solution.py:211
  18.9 2.9 %collective-permute-start.6 = (f32[72,128]{1,0:T(8,128)S(1)}, f32[72,128]{1,0:T(8,128)S(1)}, u32[]{:S(2)}, u32[]{:S(2)}) collective-permute-start(f32[72,128]{1,0:T(8,128)S(1)} %get-tuple-element.55), channel_id=1, source_target_pairs={{0,10},{1,11},{2,8},{3,9},{4,14},{5,15},{6,12},{7,13},{8,2},{9,3},... | collective-permute-start | bytes 110600 | tf_op jit(solution)/shard_map/ppermute | solution.py:25
  21.7 1.0 %collective-permute-start.7 = (f32[72,128]{1,0:T(8,128)S(1)}, f32[72,128]{1,0:T(8,128)S(1)}, u32[]{:S(2)}, u32[]{:S(2)}) collective-permute-start(f32[72,128]{1,0:T(8,128)S(1)} %get-tuple-element.55), channel_id=1, source_target_pairs={{0,8},{1,9},{2,10},{3,11},{4,12},{5,13},{6,14},{7,15},{8,0},{9,1},... | collective-permute-start | bytes 110600 | tf_op jit(solution)/shard_map/ppermute | solution.py:25
  22.8 0.5 %collective-permute-start.8 = (f32[72,128]{1,0:T(8,128)S(1)}, f32[72,128]{1,0:T(8,128)S(1)}, u32[]{:S(2)}, u32[]{:S(2)}) collective-permute-start(f32[72,128]{1,0:T(8,128)S(1)} %get-tuple-element.55), channel_id=1, source_target_pairs={{0,2},{1,3},{2,0},{3,1},{4,6},{5,7},{6,4},{7,5},{8,10},{9,11},{10,... | collective-permute-start | bytes 110600 | tf_op jit(solution)/shard_map/ppermute | solution.py:25
  23.3 2.0 %collective-permute-done.6 = f32[72,128]{1,0:T(8,128)S(1)} collective-permute-done((f32[72,128]{1,0:T(8,128)S(1)}, f32[72,128]{1,0:T(8,128)S(1)}, u32[]{:S(2)}, u32[]{:S(2)}) %collective-permute-start.6) | collective-permute-done | bytes 36896 | tf_op jit(solution)/shard_map/ppermute | solution.py:25
  25.3 1.3 %collective-permute-done.7 = f32[72,128]{1,0:T(8,128)S(1)} collective-permute-done((f32[72,128]{1,0:T(8,128)S(1)}, f32[72,128]{1,0:T(8,128)S(1)}, u32[]{:S(2)}, u32[]{:S(2)}) %collective-permute-start.7) | collective-permute-done | bytes 36896 | tf_op jit(solution)/shard_map/ppermute | solution.py:25
  26.8 0.9 %collective-permute-start.10 = (f32[72,128]{1,0:T(8,128)S(1)}, f32[72,128]{1,0:T(8,128)S(1)}, u32[]{:S(2)}, u32[]{:S(2)}) collective-permute-start(f32[72,128]{1,0:T(8,128)S(1)} %add_add_fusion), channel_id=1, source_target_pairs={{0,4},{1,5},{2,6},{3,7},{4,0},{5,1},{6,2},{7,3},{8,12},{9,13},{10,... | collective-permute-start | bytes 110600 | tf_op jit(solution)/shard_map/ppermute | solution.py:25
  27.9 1.6 %collective-permute-start.13 = (bf16[64,1280]{1,0:T(8,128)(2,1)S(1)}, bf16[64,1280]{1,0:T(8,128)(2,1)S(1)}, u32[]{:S(2)}, u32[]{:S(2)}) collective-permute-start(bf16[64,1280]{1,0:T(8,128)(2,1)S(1)} %collective-permute-done.5), channel_id=1, source_target_pairs={{0,16},{16,0},{1,17},{17,1},{2,18},{18,2},{3,19},{19,3},{4,20},{20... | collective-permute-start | bytes 491528 | tf_op jit(solution)/shard_map/ppermute | solution.py:206
  30.1 0.8 %collective-permute-done.10 = f32[72,128]{1,0:T(8,128)S(1)} collective-permute-done((f32[72,128]{1,0:T(8,128)S(1)}, f32[72,128]{1,0:T(8,128)S(1)}, u32[]{:S(2)}, u32[]{:S(2)}) %collective-permute-start.10) | collective-permute-done | bytes 36896 | tf_op jit(solution)/shard_map/ppermute | solution.py:25
  30.9 0.8 %shard_map.46 = (bf16[64,1024]{1,0:T(8,128)(2,1)S(1)}, bf16[64,1280]{1,0:T(8,128)(2,1)S(1)}) custom-call(s32[1]{0:T(128)} %bitcast.me_ref, f32[72,128]{1,0:T(8,128)S(1)} %add.27.packed_ref, bf16[128,1024]{1,0:T(8,128)(2,1)S(1)} %get-tuple-element.68.c_ref, f32[64,1024]{1,0:T(8,128)S(1)} %fusion.3.far_ref.z_ref, f32[128,1024]{1,0:T(8,128)S(1)} %fusion.4.other_ref, ...), custom_call_target="tpu_custom_call" | custom-call | tf_op jit(solution)/shard_map/pallas_call | solution.py:261
  31.6 0.6 %collective-permute-start.12 = (bf16[64,1280]{1,0:T(8,128)(2,1)S(1)}, bf16[64,1280]{1,0:T(8,128)(2,1)S(1)}, u32[]{:S(2)}, u32[]{:S(2)}) collective-permute-start(bf16[64,1280]{1,0:T(8,128)(2,1)S(1)} %get-tuple-element.72), channel_id=1, source_target_pairs={{0,2},{1,3},{2,0},{3,1},{4,6},{5,7},{6,4},{7,5},{8,10},{9,11},{10,... | collective-permute-start | bytes 491528 | tf_op jit(solution)/shard_map/ppermute | solution.py:25
  32.3 0.8 %shard_map.47 = (bf16[64,1024]{1,0:T(8,128)(2,1)S(1)}, f32[64,1280]{1,0:T(8,128)S(1)}) custom-call(s32[1]{0:T(128)} %bitcast.me_ref, f32[72,128]{1,0:T(8,128)S(1)} %add.27.packed_ref, bf16[128,1024]{1,0:T(8,128)(2,1)S(1)} %get-tuple-element.68.c_ref, f32[64,1024]{1,0:T(8,128)S(1)} %fusion.2.near_ref.z_ref, f32[128,1024]{1,0:T(8,128)S(1)} %fusion.4.other_ref, ...), custom_call_target="tpu_custom_call" | custom-call | tf_op jit(solution)/shard_map/pallas_call | solution.py:261
  33.2 1.6 %collective-permute-start.18 = (bf16[128,512]{1,0:T(8,128)(2,1)S(1)}, bf16[128,512]{1,0:T(8,128)(2,1)S(1)}, u32[]{:S(2)}, u32[]{:S(2)}) collective-permute-start(bf16[128,512]{1,0:T(8,128)(2,1)S(1)} %slice.35.refs_2_), channel_id=1, source_target_pairs={{0,16},{16,0},{1,17},{17,1},{2,18},{18,2},{3,19},{19,3},{4,20},{20... | collective-permute-start | bytes 393224 | tf_op jit(solution)/shard_map/ppermute | solution.py:206
  34.8 1.2 %collective-permute-start.20 = (bf16[128,512]{1,0:T(8,128)(2,1)S(1)}, bf16[128,512]{1,0:T(8,128)(2,1)S(1)}, u32[]{:S(2)}, u32[]{:S(2)}) collective-permute-start(bf16[128,512]{1,0:T(8,128)(2,1)S(1)} %collective-permute-done.19.refs_3_), channel_id=1, source_target_pairs={{0,16},{16,0},{1,17},{17,1},{2,18},{18,2},{3,19},{19,3},{4,20},{20... | collective-permute-start | bytes 393224 | tf_op jit(solution)/shard_map/ppermute | solution.py:206
  36.0 1.1 %collective-permute-done.12 = bf16[64,1280]{1,0:T(8,128)(2,1)S(1)} collective-permute-done((bf16[64,1280]{1,0:T(8,128)(2,1)S(1)}, bf16[64,1280]{1,0:T(8,128)(2,1)S(1)}, u32[]{:S(2)}, u32[]{:S(2)}) %collective-permute-start.12) | collective-permute-done | bytes 163872 | tf_op jit(solution)/shard_map/ppermute | solution.py:25
  37.3 2.4 %collective-permute-start.14 = (bf16[16,1280]{1,0:T(8,128)(2,1)S(1)}, bf16[16,1280]{1,0:T(8,128)(2,1)S(1)}, u32[]{:S(2)}, u32[]{:S(2)}) collective-permute-start(bf16[16,1280]{1,0:T(8,128)(2,1)S(1)} %get-tuple-element.92), channel_id=1, source_target_pairs={{0,12},{1,13},{2,14},{3,15},{4,8},{5,9},{6,10},{7,11},{8,4},{9,5},... | collective-permute-start | bytes 122888 | tf_op jit(solution)/shard_map/ppermute | solution.py:25
  39.9 1.9 %collective-permute-start.16 = (bf16[16,1280]{1,0:T(8,128)(2,1)S(1)}, bf16[16,1280]{1,0:T(8,128)(2,1)S(1)}, u32[]{:S(2)}, u32[]{:S(2)}) collective-permute-start(bf16[16,1280]{1,0:T(8,128)(2,1)S(1)} %get-tuple-element.90), channel_id=1, source_target_pairs={{0,4},{1,5},{2,6},{3,7},{4,0},{5,1},{6,2},{7,3},{8,12},{9,13},{10,... | collective-permute-start | bytes 122888 | tf_op jit(solution)/shard_map/ppermute | solution.py:25
  42.0 0.5 %shard_map.48.refs_4_ = f32[1280,512]{1,0:T(8,128)S(1)} custom-call(bf16[128,1280]{1,0:T(8,128)(2,1)S(1)} %pad_maximum_fusion.1.refs_0_, bf16[128,1280]{1,0:T(8,128)(2,1)S(1)} %collective-permute-done.11.refs_1_, bf16[128,512]{1,0:T(8,128)(2,1)S(1)} %slice.35.refs_2_, bf16[128,512]{1,0:T(8,128)(2,1)S(1)} %collective-permute-done.19.refs_3_), custom_call_target="tpu_custom_call" | custom-call | tf_op jit(solution)/shard_map/pallas_call | solution.py:271
  42.5 1.8 %shard_map.49 = f32[1280,512]{1,0:T(8,128)} custom-call(bf16[128,1280]{1,0:T(8,128)(2,1)S(1)} %constant_dynamic-update-slice_fusion.2.refs_0_, bf16[128,1280]{1,0:T(8,128)(2,1)S(1)} %collective-permute-done.17.refs_1_, bf16[128,512]{1,0:T(8,128)(2,1)S(1)} %collective-permute-done.18.refs_2_, bf16[128,512]{1,0:T(8,128)(2,1)S(1)} %collective-permute-done.20.refs_3_, ...), custom_call_target="tpu_custom_call" | custom-call | tf_op jit(solution)/shard_map/pallas_call | solution.py:301
  44.3 0.6 %collective-permute-done.15 = bf16[16,1280]{1,0:T(8,128)(2,1)S(1)} collective-permute-done((bf16[16,1280]{1,0:T(8,128)(2,1)S(1)}, bf16[16,1280]{1,0:T(8,128)(2,1)S(1)}, u32[]{:S(2)}, u32[]{:S(2)}) %collective-permute-start.15) | collective-permute-done | bytes 40992 | tf_op jit(solution)/shard_map/ppermute | solution.py:25
  45.1 1.2 %collective-permute-done.21.other_ref = f32[8,1280]{1,0:T(8,128)S(1)} collective-permute-done((f32[8,1280]{1,0:T(8,128)S(1)}, f32[8,1280]{1,0:T(8,128)S(1)}, u32[]{:S(2)}, u32[]{:S(2)}) %collective-permute-start.21) | collective-permute-done | bytes 40992 | tf_op jit(solution)/shard_map/ppermute | solution.py:25
  46.3 0.7 %shard_map.50 = f32[8,2,1280]{2,1,0:T(2,128)} custom-call(s32[1]{0:T(128)} %bitcast.me_ref, f32[8,1280]{1,0:T(8,128)S(1)} %get-tuple-element.94.own_ref, f32[8,1280]{1,0:T(8,128)S(1)} %collective-permute-done.21.other_ref), custom_call_target="tpu_custom_call" | custom-call | tf_op jit(solution)/shard_map/pallas_call | solution.py:314
  (43 shorter events, 3.4 us)
Async XLA Ops:
  0.6 1.6 %collective-permute-start = (bf16[8,2,1280]{2,1,0:T(2,128)(2,1)}, bf16[8,2,1280]{2,1,0:T(2,128)(2,1)S(1)}, u32[]{:S(2)}, u32[]{:S(2)}) collective-permute-start(bf16[8,2,1280]{2,1,0:T(2,128)(2,1)} %images_ref.1), channel_id=1, source_target_pairs={{0,1},{1,0},{2,3},{3,2},{4,5},{5,4},{6,7},{7,6},{8,9},{9,8},{10,11... | collective-permute-start | bytes 122888 | tf_op jit(solution)/shard_map/ppermute | solution.py:25
  1.1 0.8 %copy-start = (bf16[8,2,1280]{2,1,0:T(2,128)(2,1)S(1)}, bf16[8,2,1280]{2,1,0:T(2,128)(2,1)}, u32[]{:S(2)}) copy-start(bf16[8,2,1280]{2,1,0:T(2,128)(2,1)} %images_ref.1) | copy-start | bytes 122884
  2.2 5.9 %collective-permute-start.4 = (bf16[1280,512]{1,0:T(8,128)(2,1)}, bf16[1280,512]{1,0:T(8,128)(2,1)S(1)}, u32[]{:S(2)}, u32[]{:S(2)}) collective-permute-start(bf16[1280,512]{1,0:T(8,128)(2,1)} %param.3), channel_id=1, source_target_pairs={{0,1},{1,0},{2,3},{3,2},{4,5},{5,4},{6,7},{7,6},{8,9},{9,8},{10,11... | collective-permute-start | bytes 3932168 | tf_op jit(solution)/shard_map/ppermute | solution.py:25
  2.6 7.2 %collective-permute-start.1 = (bf16[16,1280]{1,0:T(8,128)(2,1)S(1)}, bf16[16,1280]{1,0:T(8,128)(2,1)S(1)}, u32[]{:S(2)}, u32[]{:S(2)}) collective-permute-start(bf16[16,1280]{1,0:T(8,128)(2,1)S(1)} %shard_map.42), channel_id=1, source_target_pairs={{0,12},{1,13},{2,14},{3,15},{4,8},{5,9},{6,10},{7,11},{8,4},{9,5},... | collective-permute-start | bytes 122888 | tf_op jit(solution)/shard_map/ppermute | solution.py:25
  7.4 4.9 %collective-permute-start.2 = (bf16[16,1280]{1,0:T(8,128)(2,1)S(1)}, bf16[16,1280]{1,0:T(8,128)(2,1)S(1)}, u32[]{:S(2)}, u32[]{:S(2)}) collective-permute-start(bf16[16,1280]{1,0:T(8,128)(2,1)S(1)} %shard_map.42), channel_id=1, source_target_pairs={{0,8},{1,9},{2,10},{3,11},{4,12},{5,13},{6,14},{7,15},{8,0},{9,1},... | collective-permute-start | bytes 122888 | tf_op jit(solution)/shard_map/ppermute | solution.py:25
  7.4 4.9 %collective-permute-start.3 = (bf16[16,1280]{1,0:T(8,128)(2,1)S(1)}, bf16[16,1280]{1,0:T(8,128)(2,1)S(1)}, u32[]{:S(2)}, u32[]{:S(2)}) collective-permute-start(bf16[16,1280]{1,0:T(8,128)(2,1)S(1)} %shard_map.42), channel_id=1, source_target_pairs={{0,4},{1,5},{2,6},{3,7},{4,0},{5,1},{6,2},{7,3},{8,12},{9,13},{10,... | collective-permute-start | bytes 122888 | tf_op jit(solution)/shard_map/ppermute | solution.py:25
  12.4 5.5 %collective-permute-start.5 = (bf16[64,1280]{1,0:T(8,128)(2,1)S(1)}, bf16[64,1280]{1,0:T(8,128)(2,1)S(1)}, u32[]{:S(2)}, u32[]{:S(2)}) collective-permute-start(bf16[64,1280]{1,0:T(8,128)(2,1)S(1)} %pad_maximum_fusion.2), channel_id=1, source_target_pairs={{0,2},{1,3},{2,0},{3,1},{4,6},{5,7},{6,4},{7,5},{8,10},{9,11},{10,... | collective-permute-start | bytes 491528 | tf_op jit(solution)/shard_map/ppermute | solution.py:25
  14.6 12.1 %collective-permute-start.9 = (bf16[64,1280]{1,0:T(8,128)(2,1)S(1)}, bf16[64,1280]{1,0:T(8,128)(2,1)S(1)}, u32[]{:S(2)}, u32[]{:S(2)}) collective-permute-start(bf16[64,1280]{1,0:T(8,128)(2,1)S(1)} %pad_maximum_fusion.2), channel_id=1, source_target_pairs={{0,16},{16,0},{1,17},{17,1},{2,18},{18,2},{3,19},{19,3},{4,20},{20... | collective-permute-start | bytes 491528 | tf_op jit(solution)/shard_map/ppermute | solution.py:206
  18.9 6.4 %collective-permute-start.6 = (f32[72,128]{1,0:T(8,128)S(1)}, f32[72,128]{1,0:T(8,128)S(1)}, u32[]{:S(2)}, u32[]{:S(2)}) collective-permute-start(f32[72,128]{1,0:T(8,128)S(1)} %get-tuple-element.55), channel_id=1, source_target_pairs={{0,10},{1,11},{2,8},{3,9},{4,14},{5,15},{6,12},{7,13},{8,2},{9,3},... | collective-permute-start | bytes 110600 | tf_op jit(solution)/shard_map/ppermute | solution.py:25
  21.7 4.9 %collective-permute-start.7 = (f32[72,128]{1,0:T(8,128)S(1)}, f32[72,128]{1,0:T(8,128)S(1)}, u32[]{:S(2)}, u32[]{:S(2)}) collective-permute-start(f32[72,128]{1,0:T(8,128)S(1)} %get-tuple-element.55), channel_id=1, source_target_pairs={{0,8},{1,9},{2,10},{3,11},{4,12},{5,13},{6,14},{7,15},{8,0},{9,1},... | collective-permute-start | bytes 110600 | tf_op jit(solution)/shard_map/ppermute | solution.py:25
  22.8 4.0 %collective-permute-start.8 = (f32[72,128]{1,0:T(8,128)S(1)}, f32[72,128]{1,0:T(8,128)S(1)}, u32[]{:S(2)}, u32[]{:S(2)}) collective-permute-start(f32[72,128]{1,0:T(8,128)S(1)} %get-tuple-element.55), channel_id=1, source_target_pairs={{0,2},{1,3},{2,0},{3,1},{4,6},{5,7},{6,4},{7,5},{8,10},{9,11},{10,... | collective-permute-start | bytes 110600 | tf_op jit(solution)/shard_map/ppermute | solution.py:25
  26.7 2.8 %collective-permute-start.11 = (bf16[128,1280]{1,0:T(8,128)(2,1)S(1)}, bf16[128,1280]{1,0:T(8,128)(2,1)S(1)}, u32[]{:S(2)}, u32[]{:S(2)}) collective-permute-start(bf16[128,1280]{1,0:T(8,128)(2,1)S(1)} %pad_maximum_fusion.1.refs_0_), channel_id=1, source_target_pairs={{0,1},{1,0},{2,3},{3,2},{4,5},{5,4},{6,7},{7,6},{8,9},{9,8},{10,11... | collective-permute-start | bytes 983048 | tf_op jit(solution)/shard_map/ppermute | solution.py:25
  26.8 4.0 %collective-permute-start.10 = (f32[72,128]{1,0:T(8,128)S(1)}, f32[72,128]{1,0:T(8,128)S(1)}, u32[]{:S(2)}, u32[]{:S(2)}) collective-permute-start(f32[72,128]{1,0:T(8,128)S(1)} %add_add_fusion), channel_id=1, source_target_pairs={{0,4},{1,5},{2,6},{3,7},{4,0},{5,1},{6,2},{7,3},{8,12},{9,13},{10,... | collective-permute-start | bytes 110600 | tf_op jit(solution)/shard_map/ppermute | solution.py:25
  27.9 9.2 %collective-permute-start.13 = (bf16[64,1280]{1,0:T(8,128)(2,1)S(1)}, bf16[64,1280]{1,0:T(8,128)(2,1)S(1)}, u32[]{:S(2)}, u32[]{:S(2)}) collective-permute-start(bf16[64,1280]{1,0:T(8,128)(2,1)S(1)} %collective-permute-done.5), channel_id=1, source_target_pairs={{0,16},{16,0},{1,17},{17,1},{2,18},{18,2},{3,19},{19,3},{4,20},{20... | collective-permute-start | bytes 491528 | tf_op jit(solution)/shard_map/ppermute | solution.py:206
  31.6 5.5 %collective-permute-start.12 = (bf16[64,1280]{1,0:T(8,128)(2,1)S(1)}, bf16[64,1280]{1,0:T(8,128)(2,1)S(1)}, u32[]{:S(2)}, u32[]{:S(2)}) collective-permute-start(bf16[64,1280]{1,0:T(8,128)(2,1)S(1)} %get-tuple-element.72), channel_id=1, source_target_pairs={{0,2},{1,3},{2,0},{3,1},{4,6},{5,7},{6,4},{7,5},{8,10},{9,11},{10,... | collective-permute-start | bytes 491528 | tf_op jit(solution)/shard_map/ppermute | solution.py:25
  33.1 1.7 %collective-permute-start.19 = (bf16[128,512]{1,0:T(8,128)(2,1)S(1)}, bf16[128,512]{1,0:T(8,128)(2,1)S(1)}, u32[]{:S(2)}, u32[]{:S(2)}) collective-permute-start(bf16[128,512]{1,0:T(8,128)(2,1)S(1)} %slice.42), channel_id=1, source_target_pairs={{0,1},{1,0},{2,3},{3,2},{4,5},{5,4},{6,7},{7,6},{8,9},{9,8},{10,11... | collective-permute-start | bytes 393224 | tf_op jit(solution)/shard_map/ppermute | solution.py:25
  33.2 6.7 %collective-permute-start.18 = (bf16[128,512]{1,0:T(8,128)(2,1)S(1)}, bf16[128,512]{1,0:T(8,128)(2,1)S(1)}, u32[]{:S(2)}, u32[]{:S(2)}) collective-permute-start(bf16[128,512]{1,0:T(8,128)(2,1)S(1)} %slice.35.refs_2_), channel_id=1, source_target_pairs={{0,16},{16,0},{1,17},{17,1},{2,18},{18,2},{3,19},{19,3},{4,20},{20... | collective-permute-start | bytes 393224 | tf_op jit(solution)/shard_map/ppermute | solution.py:206
  34.8 7.2 %collective-permute-start.20 = (bf16[128,512]{1,0:T(8,128)(2,1)S(1)}, bf16[128,512]{1,0:T(8,128)(2,1)S(1)}, u32[]{:S(2)}, u32[]{:S(2)}) collective-permute-start(bf16[128,512]{1,0:T(8,128)(2,1)S(1)} %collective-permute-done.19.refs_3_), channel_id=1, source_target_pairs={{0,16},{16,0},{1,17},{17,1},{2,18},{18,2},{3,19},{19,3},{4,20},{20... | collective-permute-start | bytes 393224 | tf_op jit(solution)/shard_map/ppermute | solution.py:206
  37.2 5.3 %collective-permute-start.17 = (bf16[128,1280]{1,0:T(8,128)(2,1)S(1)}, bf16[128,1280]{1,0:T(8,128)(2,1)S(1)}, u32[]{:S(2)}, u32[]{:S(2)}) collective-permute-start(bf16[128,1280]{1,0:T(8,128)(2,1)S(1)} %constant_dynamic-update-slice_fusion.2.refs_0_), channel_id=1, source_target_pairs={{0,1},{1,0},{2,3},{3,2},{4,5},{5,4},{6,7},{7,6},{8,9},{9,8},{10,11... | collective-permute-start | bytes 983048 | tf_op jit(solution)/shard_map/ppermute | solution.py:25
  37.3 7.0 %collective-permute-start.14 = (bf16[16,1280]{1,0:T(8,128)(2,1)S(1)}, bf16[16,1280]{1,0:T(8,128)(2,1)S(1)}, u32[]{:S(2)}, u32[]{:S(2)}) collective-permute-start(bf16[16,1280]{1,0:T(8,128)(2,1)S(1)} %get-tuple-element.92), channel_id=1, source_target_pairs={{0,12},{1,13},{2,14},{3,15},{4,8},{5,9},{6,10},{7,11},{8,4},{9,5},... | collective-permute-start | bytes 122888 | tf_op jit(solution)/shard_map/ppermute | solution.py:25
  39.7 5.2 %collective-permute-start.15 = (bf16[16,1280]{1,0:T(8,128)(2,1)S(1)}, bf16[16,1280]{1,0:T(8,128)(2,1)S(1)}, u32[]{:S(2)}, u32[]{:S(2)}) collective-permute-start(bf16[16,1280]{1,0:T(8,128)(2,1)S(1)} %get-tuple-element.91), channel_id=1, source_target_pairs={{0,8},{1,9},{2,10},{3,11},{4,12},{5,13},{6,14},{7,15},{8,0},{9,1},... | collective-permute-start | bytes 122888 | tf_op jit(solution)/shard_map/ppermute | solution.py:25
  39.9 5.1 %collective-permute-start.16 = (bf16[16,1280]{1,0:T(8,128)(2,1)S(1)}, bf16[16,1280]{1,0:T(8,128)(2,1)S(1)}, u32[]{:S(2)}, u32[]{:S(2)}) collective-permute-start(bf16[16,1280]{1,0:T(8,128)(2,1)S(1)} %get-tuple-element.90), channel_id=1, source_target_pairs={{0,4},{1,5},{2,6},{3,7},{4,0},{5,1},{6,2},{7,3},{8,12},{9,13},{10,... | collective-permute-start | bytes 122888 | tf_op jit(solution)/shard_map/ppermute | solution.py:25
  45.0 1.3 %collective-permute-start.21 = (f32[8,1280]{1,0:T(8,128)S(1)}, f32[8,1280]{1,0:T(8,128)S(1)}, u32[]{:S(2)}, u32[]{:S(2)}) collective-permute-start(f32[8,1280]{1,0:T(8,128)S(1)} %get-tuple-element.93), channel_id=1, source_target_pairs={{0,1},{1,0},{2,3},{3,2},{4,5},{5,4},{6,7},{7,6},{8,9},{9,8},{10,11... | collective-permute-start | bytes 122888 | tf_op jit(solution)/shard_map/ppermute | solution.py:25

commit v2 on v1

--- a/solution.py
+++ b/solution.py
@@ -235,11 +235,9 @@
         [pltpu.VMEM((owners, own, width), F32)],
     )(me, near, far)
 
-    top = owners // 2
-    along, beside, corner = (swap(packed, "dp", bits) for bits in (ACROSS, top, ACROSS | top))
-    corner, beside, along, wide_t = lax.optimization_barrier((corner, beside, along, wide_t))
-    along, near_others = lax.optimization_barrier((along, near_others))
-    packed = (packed + along) + (beside + corner)
+    along = swap(packed, "dp", ACROSS)
+    along, wide_t, near_others = lax.optimization_barrier((along, wide_t, near_others))
+    packed = packed + along
     packed, near_late, far_late, rows = lax.optimization_barrier(
         (packed, near, far, jnp.concatenate([column, across], axis=0))
     )
@@ -250,12 +248,9 @@
     base, sent = lax.optimization_barrier((base, across))
     far_others = over_rep(sent)
     other = matmul(rows_core, wide)
-    bit = QUAD
-    while bit < top:
-        received = swap(packed, "dp", bit)
-        received, other, base = lax.optimization_barrier((received, other, base))
-        packed = packed + received
-        bit *= 2
+    received = [swap(packed, "dp", high * QUAD) for high in range(outer - 1, 0, -1)]
+    received, other, base = lax.optimization_barrier((received, other, base))
+    packed = (packed + received[-1]) + functools.reduce(jnp.add, received[:-1])
 
     def grads(side, z, kind):
         return call(

time: 47.1 us -> 47.2 us (level)
  starting transfers between devices: 24.5 us -> 25.8 us
  waiting for transfers between devices: 11.2 us -> 9.97 us
    ppermute x18, waiting for transfers between devices: 11 us -> 9.11 us  [swap(): lax.ppermute(block, axis, [(i, i ^ bits) for i in range(lax.axis_size(axi...]
    ppermute x18, starting transfers between devices: 18.6 us -> 19.8 us  [swap(): lax.ppermute(block, axis, [(i, i ^ bits) for i in range(lax.axis_size(axi...]
    ppermute x4, waiting for transfers between devices: 0.22 us -> 0.86 us  [over_rep(): lax.ppermute(array, 'rep', [(i, (i + shift) % groups) for i in range(grou...]
  transfers between devices with their start and end apart: 22 -> 22, of which waited for: 11 -> 10; matrix products, arithmetic and copies ran while one was open for 7% -> 7% of each run, Pallas kernels for 11% -> 11%
where the time goes in v2:
time: 47.2 us; the launch traced here: 47 us
  starting transfers between devices  25.8 us (55%)
  waiting for transfers between devices  9.97 us (21%)
  Pallas kernels  5.96 us (13%)
  other arithmetic  1.8 us (4%)
  matrix products  1.68 us (4%)
  between operations  0.88 us (2%)
  local copies, waits for them, and re-layouts  0.86 us (2%)
    ppermute x18, starting transfers between devices, swap(): lax.ppermute(block, axis, [(i, i ^ bits) for i in range(lax.axis_size(axi...  19.8 us
    ppermute x18, waiting for transfers between devices, swap(): lax.ppermute(block, axis, [(i, i ^ bits) for i in range(lax.axis_size(axi...  9.11 us
    ppermute x4, starting transfers between devices, over_rep(): lax.ppermute(array, 'rep', [(i, (i + shift) % groups) for i in range(grou...  5.98 us
    pallas_call x1, Pallas kernels, shards(): call(last_weight_kernel, struct((depth, block), F32), [VMEM] * 5, [pltpu....  1.79 us
    dot_general x3, matrix products, matmul(): return jnp.dot(rows, matrix, preferred_element_type=F32)  1.68 us
    concatenate x1, other arithmetic, shards(): wide = jnp.concatenate([weight, weight_core], axis=1)  1.67 us
    pallas_call x2, Pallas kernels, grads(): call(functools.partial(grads_kernel, side, scale, features), (struct((hal...  1.57 us
  transfers between devices with their start and end apart: 22, of which 10 were waited for; matrix products, arithmetic and copies ran while one was open for 7% of the time, Pallas kernels for 11%

profile of v2, /device:TPU:0, one launch (start us, length us, event | category | flops | bytes accessed | tf_op | source)
XLA Modules:
  0.0 47.0 jit_solution(2392074798752982937)
XLA Ops:
  0.6 0.5 %collective-permute-start = (bf16[8,2,1280]{2,1,0:T(2,128)(2,1)}, bf16[8,2,1280]{2,1,0:T(2,128)(2,1)S(1)}, u32[]{:S(2)}, u32[]{:S(2)}) collective-permute-start(bf16[8,2,1280]{2,1,0:T(2,128)(2,1)} %images_ref.1), channel_id=1, source_target_pairs={{0,1},{1,0},{2,3},{3,2},{4,5},{5,4},{6,7},{7,6},{8,9},{9,8},{10,11... | collective-permute-start | bytes 122888 | tf_op jit(solution)/shard_map/ppermute | solution.py:25
  1.1 0.8 %copy-done = bf16[8,2,1280]{2,1,0:T(2,128)(2,1)S(1)} copy-done((bf16[8,2,1280]{2,1,0:T(2,128)(2,1)S(1)}, bf16[8,2,1280]{2,1,0:T(2,128)(2,1)}, u32[]{:S(2)}) %copy-start) | copy-done | bytes 40984
  2.6 4.8 %collective-permute-start.1 = (bf16[16,1280]{1,0:T(8,128)(2,1)S(1)}, bf16[16,1280]{1,0:T(8,128)(2,1)S(1)}, u32[]{:S(2)}, u32[]{:S(2)}) collective-permute-start(bf16[16,1280]{1,0:T(8,128)(2,1)S(1)} %shard_map.42), channel_id=1, source_target_pairs={{0,12},{1,13},{2,14},{3,15},{4,8},{5,9},{6,10},{7,11},{8,4},{9,5},... | collective-permute-start | bytes 122888 | tf_op jit(solution)/shard_map/ppermute | solution.py:25
  7.4 0.6 %collective-permute-start.3 = (bf16[16,1280]{1,0:T(8,128)(2,1)S(1)}, bf16[16,1280]{1,0:T(8,128)(2,1)S(1)}, u32[]{:S(2)}, u32[]{:S(2)}) collective-permute-start(bf16[16,1280]{1,0:T(8,128)(2,1)S(1)} %shard_map.42), channel_id=1, source_target_pairs={{0,4},{1,5},{2,6},{3,7},{4,0},{5,1},{6,2},{7,3},{8,12},{9,13},{10,... | collective-permute-start | bytes 122888 | tf_op jit(solution)/shard_map/ppermute | solution.py:25
  8.1 1.7 %pad_maximum_fusion.wide_ref = bf16[1280,1024]{1,0:T(8,128)(2,1)S(1)} fusion(bf16[1280,512]{1,0:T(8,128)(2,1)S(1)} %collective-permute-done.4, bf16[1280,512]{1,0:T(8,128)(2,1)} %param.3), kind=kLoop, calls=%fused_computation | loop fusion | flops 5242880 | bytes 5242880 | tf_op jit(solution)/shard_map/concatenate | solution.py:219
  9.8 2.6 %collective-permute-done.2 = bf16[16,1280]{1,0:T(8,128)(2,1)S(1)} collective-permute-done((bf16[16,1280]{1,0:T(8,128)(2,1)S(1)}, bf16[16,1280]{1,0:T(8,128)(2,1)S(1)}, u32[]{:S(2)}, u32[]{:S(2)}) %collective-permute-start.2) | collective-permute-done | bytes 40992 | tf_op jit(solution)/shard_map/ppermute | solution.py:25
  12.4 1.6 %collective-permute-start.5 = (bf16[64,1280]{1,0:T(8,128)(2,1)S(1)}, bf16[64,1280]{1,0:T(8,128)(2,1)S(1)}, u32[]{:S(2)}, u32[]{:S(2)}) collective-permute-start(bf16[64,1280]{1,0:T(8,128)(2,1)S(1)} %pad_maximum_fusion.2), channel_id=1, source_target_pairs={{0,2},{1,3},{2,0},{3,1},{4,6},{5,7},{6,4},{7,5},{8,10},{9,11},{10,... | collective-permute-start | bytes 491528 | tf_op jit(solution)/shard_map/ppermute | solution.py:25
  13.9 0.7 %shard_map.44.w_ref = bf16[1024,1280]{1,0:T(8,128)(2,1)S(1)} custom-call(bf16[1280,1024]{1,0:T(8,128)(2,1)S(1)} %pad_maximum_fusion.wide_ref), custom_call_target="tpu_custom_call" | custom-call | tf_op jit(solution)/shard_map/pallas_call | solution.py:225
  14.6 1.6 %collective-permute-start.7 = (bf16[64,1280]{1,0:T(8,128)(2,1)S(1)}, bf16[64,1280]{1,0:T(8,128)(2,1)S(1)}, u32[]{:S(2)}, u32[]{:S(2)}) collective-permute-start(bf16[64,1280]{1,0:T(8,128)(2,1)S(1)} %pad_maximum_fusion.2), channel_id=1, source_target_pairs={{0,16},{16,0},{1,17},{17,1},{2,18},{18,2},{3,19},{19,3},{4,20},{20... | collective-permute-start | bytes 491528 | tf_op jit(solution)/shard_map/ppermute | solution.py:206
  16.2 0.6 %fusion.2.near_ref.z_ref = f32[64,1024]{1,0:T(8,128)S(1)} fusion(bf16[64,1280]{1,0:T(8,128)(2,1)S(1)} %pad_maximum_fusion.2, bf16[1280,1024]{1,0:T(8,128)(2,1)S(1)} %pad_maximum_fusion.wide_ref), kind=kOutput, calls=%fused_computation.12 | convolution fusion | flops 167772160 | bytes 3047424 | tf_op jit(solution)/shard_map/dot_general | solution.py:211
  16.8 1.1 %collective-permute-done.5 = bf16[64,1280]{1,0:T(8,128)(2,1)S(1)} collective-permute-done((bf16[64,1280]{1,0:T(8,128)(2,1)S(1)}, bf16[64,1280]{1,0:T(8,128)(2,1)S(1)}, u32[]{:S(2)}, u32[]{:S(2)}) %collective-permute-start.5) | collective-permute-done | bytes 163872 | tf_op jit(solution)/shard_map/ppermute | solution.py:25
  17.9 0.6 %fusion.3.far_ref.z_ref = f32[64,1024]{1,0:T(8,128)S(1)} fusion(bf16[64,1280]{1,0:T(8,128)(2,1)S(1)} %collective-permute-done.5, bf16[1280,1024]{1,0:T(8,128)(2,1)S(1)} %pad_maximum_fusion.wide_ref), kind=kOutput, calls=%fused_computation.13 | convolution fusion | flops 167772160 | bytes 3047424 | tf_op jit(solution)/shard_map/dot_general | solution.py:211
  18.9 1.6 %collective-permute-start.6 = (f32[72,128]{1,0:T(8,128)S(1)}, f32[72,128]{1,0:T(8,128)S(1)}, u32[]{:S(2)}, u32[]{:S(2)}) collective-permute-start(f32[72,128]{1,0:T(8,128)S(1)} %get-tuple-element.54), channel_id=1, source_target_pairs={{0,2},{1,3},{2,0},{3,1},{4,6},{5,7},{6,4},{7,5},{8,10},{9,11},{10,... | collective-permute-start | bytes 110600 | tf_op jit(solution)/shard_map/ppermute | solution.py:25
  20.4 2.4 %collective-permute-done.6 = f32[72,128]{1,0:T(8,128)S(1)} collective-permute-done((f32[72,128]{1,0:T(8,128)S(1)}, f32[72,128]{1,0:T(8,128)S(1)}, u32[]{:S(2)}, u32[]{:S(2)}) %collective-permute-start.6) | collective-permute-done | bytes 36896 | tf_op jit(solution)/shard_map/ppermute | solution.py:25
  22.9 2.3 %collective-permute-start.8 = (f32[72,128]{1,0:T(8,128)S(1)}, f32[72,128]{1,0:T(8,128)S(1)}, u32[]{:S(2)}, u32[]{:S(2)}) collective-permute-start(f32[72,128]{1,0:T(8,128)S(1)} %add.24), channel_id=1, source_target_pairs={{0,12},{1,13},{2,14},{3,15},{4,8},{5,9},{6,10},{7,11},{8,4},{9,5},... | collective-permute-start | bytes 110600 | tf_op jit(solution)/shard_map/ppermute | solution.py:25
  25.2 2.2 %collective-permute-start.10 = (f32[72,128]{1,0:T(8,128)S(1)}, f32[72,128]{1,0:T(8,128)S(1)}, u32[]{:S(2)}, u32[]{:S(2)}) collective-permute-start(f32[72,128]{1,0:T(8,128)S(1)} %add.24), channel_id=1, source_target_pairs={{0,4},{1,5},{2,6},{3,7},{4,0},{5,1},{6,2},{7,3},{8,12},{9,13},{10,... | collective-permute-start | bytes 110600 | tf_op jit(solution)/shard_map/ppermute | solution.py:25
  27.6 1.6 %collective-permute-start.13 = (bf16[64,1280]{1,0:T(8,128)(2,1)S(1)}, bf16[64,1280]{1,0:T(8,128)(2,1)S(1)}, u32[]{:S(2)}, u32[]{:S(2)}) collective-permute-start(bf16[64,1280]{1,0:T(8,128)(2,1)S(1)} %collective-permute-done.5), channel_id=1, source_target_pairs={{0,16},{16,0},{1,17},{17,1},{2,18},{18,2},{3,19},{19,3},{4,20},{20... | collective-permute-start | bytes 491528 | tf_op jit(solution)/shard_map/ppermute | solution.py:206
  29.2 0.5 %fusion.4.other_ref = f32[128,1024]{1,0:T(8,128)S(1)} fusion(bf16[128,1280]{1,0:T(8,128)(2,1)S(1)} %collective-permute-done.11.refs_1_, bf16[1280,1024]{1,0:T(8,128)(2,1)S(1)} %pad_maximum_fusion.wide_ref), kind=kOutput, calls=%fused_computation.14 | convolution fusion | flops 335544320 | bytes 3473408 | tf_op jit(solution)/shard_map/dot_general | solution.py:211
  29.7 0.6 %collective-permute-done.9 = f32[72,128]{1,0:T(8,128)S(1)} collective-permute-done((f32[72,128]{1,0:T(8,128)S(1)}, f32[72,128]{1,0:T(8,128)S(1)}, u32[]{:S(2)}, u32[]{:S(2)}) %collective-permute-start.9) | collective-permute-done | bytes 36896 | tf_op jit(solution)/shard_map/ppermute | solution.py:25
  30.3 0.8 %shard_map.46 = (bf16[64,1024]{1,0:T(8,128)(2,1)S(1)}, bf16[64,1280]{1,0:T(8,128)(2,1)S(1)}) custom-call(s32[1]{0:T(128)} %bitcast.me_ref, f32[72,128]{1,0:T(8,128)S(1)} %add_add_fusion.packed_ref, bf16[128,1024]{1,0:T(8,128)(2,1)S(1)} %get-tuple-element.66.c_ref, f32[64,1024]{1,0:T(8,128)S(1)} %fusion.3.far_ref.z_ref, f32[128,1024]{1,0:T(8,128)S(1)} %fusion.4.other_ref, ...), custom_call_target="tpu_custom_call" | custom-call | tf_op jit(solution)/shard_map/pallas_call | solution.py:256
  31.1 1.5 %collective-permute-start.12 = (bf16[64,1280]{1,0:T(8,128)(2,1)S(1)}, bf16[64,1280]{1,0:T(8,128)(2,1)S(1)}, u32[]{:S(2)}, u32[]{:S(2)}) collective-permute-start(bf16[64,1280]{1,0:T(8,128)(2,1)S(1)} %get-tuple-element.70), channel_id=1, source_target_pairs={{0,2},{1,3},{2,0},{3,1},{4,6},{5,7},{6,4},{7,5},{8,10},{9,11},{10,... | collective-permute-start | bytes 491528 | tf_op jit(solution)/shard_map/ppermute | solution.py:25
  32.7 0.8 %shard_map.47 = (bf16[64,1024]{1,0:T(8,128)(2,1)S(1)}, f32[64,1280]{1,0:T(8,128)S(1)}) custom-call(s32[1]{0:T(128)} %bitcast.me_ref, f32[72,128]{1,0:T(8,128)S(1)} %add_add_fusion.packed_ref, bf16[128,1024]{1,0:T(8,128)(2,1)S(1)} %get-tuple-element.66.c_ref, f32[64,1024]{1,0:T(8,128)S(1)} %fusion.2.near_ref.z_ref, f32[128,1024]{1,0:T(8,128)S(1)} %fusion.4.other_ref, ...), custom_call_target="tpu_custom_call" | custom-call | tf_op jit(solution)/shard_map/pallas_call | solution.py:256
  33.6 1.6 %collective-permute-start.18 = (bf16[128,512]{1,0:T(8,128)(2,1)S(1)}, bf16[128,512]{1,0:T(8,128)(2,1)S(1)}, u32[]{:S(2)}, u32[]{:S(2)}) collective-permute-start(bf16[128,512]{1,0:T(8,128)(2,1)S(1)} %slice.35.refs_2_), channel_id=1, source_target_pairs={{0,16},{16,0},{1,17},{17,1},{2,18},{18,2},{3,19},{19,3},{4,20},{20... | collective-permute-start | bytes 393224 | tf_op jit(solution)/shard_map/ppermute | solution.py:206
  35.2 1.2 %collective-permute-start.20 = (bf16[128,512]{1,0:T(8,128)(2,1)S(1)}, bf16[128,512]{1,0:T(8,128)(2,1)S(1)}, u32[]{:S(2)}, u32[]{:S(2)}) collective-permute-start(bf16[128,512]{1,0:T(8,128)(2,1)S(1)} %collective-permute-done.19.refs_3_), channel_id=1, source_target_pairs={{0,16},{16,0},{1,17},{17,1},{2,18},{18,2},{3,19},{19,3},{4,20},{20... | collective-permute-start | bytes 393224 | tf_op jit(solution)/shard_map/ppermute | solution.py:206
  36.4 0.8 %collective-permute-done.12 = bf16[64,1280]{1,0:T(8,128)(2,1)S(1)} collective-permute-done((bf16[64,1280]{1,0:T(8,128)(2,1)S(1)}, bf16[64,1280]{1,0:T(8,128)(2,1)S(1)}, u32[]{:S(2)}, u32[]{:S(2)}) %collective-permute-start.12) | collective-permute-done | bytes 163872 | tf_op jit(solution)/shard_map/ppermute | solution.py:25
  37.4 2.3 %collective-permute-start.14 = (bf16[16,1280]{1,0:T(8,128)(2,1)S(1)}, bf16[16,1280]{1,0:T(8,128)(2,1)S(1)}, u32[]{:S(2)}, u32[]{:S(2)}) collective-permute-start(bf16[16,1280]{1,0:T(8,128)(2,1)S(1)} %get-tuple-element.90), channel_id=1, source_target_pairs={{0,12},{1,13},{2,14},{3,15},{4,8},{5,9},{6,10},{7,11},{8,4},{9,5},... | collective-permute-start | bytes 122888 | tf_op jit(solution)/shard_map/ppermute | solution.py:25
  40.0 1.9 %collective-permute-start.16 = (bf16[16,1280]{1,0:T(8,128)(2,1)S(1)}, bf16[16,1280]{1,0:T(8,128)(2,1)S(1)}, u32[]{:S(2)}, u32[]{:S(2)}) collective-permute-start(bf16[16,1280]{1,0:T(8,128)(2,1)S(1)} %get-tuple-element.88), channel_id=1, source_target_pairs={{0,4},{1,5},{2,6},{3,7},{4,0},{5,1},{6,2},{7,3},{8,12},{9,13},{10,... | collective-permute-start | bytes 122888 | tf_op jit(solution)/shard_map/ppermute | solution.py:25
  41.8 0.5 %collective-permute-done.20.refs_3_ = bf16[128,512]{1,0:T(8,128)(2,1)S(1)} collective-permute-done((bf16[128,512]{1,0:T(8,128)(2,1)S(1)}, bf16[128,512]{1,0:T(8,128)(2,1)S(1)}, u32[]{:S(2)}, u32[]{:S(2)}) %collective-permute-start.20) | collective-permute-done | bytes 131104 | tf_op jit(solution)/shard_map/ppermute | solution.py:206
  42.4 0.5 %shard_map.48.refs_4_ = f32[1280,512]{1,0:T(8,128)S(1)} custom-call(bf16[128,1280]{1,0:T(8,128)(2,1)S(1)} %pad_maximum_fusion.1.refs_0_, bf16[128,1280]{1,0:T(8,128)(2,1)S(1)} %collective-permute-done.11.refs_1_, bf16[128,512]{1,0:T(8,128)(2,1)S(1)} %slice.35.refs_2_, bf16[128,512]{1,0:T(8,128)(2,1)S(1)} %collective-permute-done.19.refs_3_), custom_call_target="tpu_custom_call" | custom-call | tf_op jit(solution)/shard_map/pallas_call | solution.py:266
  42.9 1.8 %shard_map.49 = f32[1280,512]{1,0:T(8,128)} custom-call(bf16[128,1280]{1,0:T(8,128)(2,1)S(1)} %constant_dynamic-update-slice_fusion.2.refs_0_, bf16[128,1280]{1,0:T(8,128)(2,1)S(1)} %collective-permute-done.17.refs_1_, bf16[128,512]{1,0:T(8,128)(2,1)S(1)} %collective-permute-done.18.refs_2_, bf16[128,512]{1,0:T(8,128)(2,1)S(1)} %collective-permute-done.20.refs_3_, ...), custom_call_target="tpu_custom_call" | custom-call | tf_op jit(solution)/shard_map/pallas_call | solution.py:296
  45.1 1.2 %collective-permute-done.21.other_ref = f32[8,1280]{1,0:T(8,128)S(1)} collective-permute-done((f32[8,1280]{1,0:T(8,128)S(1)}, f32[8,1280]{1,0:T(8,128)S(1)}, u32[]{:S(2)}, u32[]{:S(2)}) %collective-permute-start.21) | collective-permute-done | bytes 40992 | tf_op jit(solution)/shard_map/ppermute | solution.py:25
  46.3 0.7 %shard_map.50 = f32[8,2,1280]{2,1,0:T(2,128)} custom-call(s32[1]{0:T(128)} %bitcast.me_ref, f32[8,1280]{1,0:T(8,128)S(1)} %get-tuple-element.92.own_ref, f32[8,1280]{1,0:T(8,128)S(1)} %collective-permute-done.21.other_ref), custom_call_target="tpu_custom_call" | custom-call | tf_op jit(solution)/shard_map/pallas_call | solution.py:309
  (43 shorter events, 2.4 us)
Async XLA Ops:
  0.6 1.6 %collective-permute-start = (bf16[8,2,1280]{2,1,0:T(2,128)(2,1)}, bf16[8,2,1280]{2,1,0:T(2,128)(2,1)S(1)}, u32[]{:S(2)}, u32[]{:S(2)}) collective-permute-start(bf16[8,2,1280]{2,1,0:T(2,128)(2,1)} %images_ref.1), channel_id=1, source_target_pairs={{0,1},{1,0},{2,3},{3,2},{4,5},{5,4},{6,7},{7,6},{8,9},{9,8},{10,11... | collective-permute-start | bytes 122888 | tf_op jit(solution)/shard_map/ppermute | solution.py:25
  1.1 0.8 %copy-start = (bf16[8,2,1280]{2,1,0:T(2,128)(2,1)S(1)}, bf16[8,2,1280]{2,1,0:T(2,128)(2,1)}, u32[]{:S(2)}) copy-start(bf16[8,2,1280]{2,1,0:T(2,128)(2,1)} %images_ref.1) | copy-start | bytes 122884
  2.2 5.9 %collective-permute-start.4 = (bf16[1280,512]{1,0:T(8,128)(2,1)}, bf16[1280,512]{1,0:T(8,128)(2,1)S(1)}, u32[]{:S(2)}, u32[]{:S(2)}) collective-permute-start(bf16[1280,512]{1,0:T(8,128)(2,1)} %param.3), channel_id=1, source_target_pairs={{0,1},{1,0},{2,3},{3,2},{4,5},{5,4},{6,7},{7,6},{8,9},{9,8},{10,11... | collective-permute-start | bytes 3932168 | tf_op jit(solution)/shard_map/ppermute | solution.py:25
  2.6 7.2 %collective-permute-start.1 = (bf16[16,1280]{1,0:T(8,128)(2,1)S(1)}, bf16[16,1280]{1,0:T(8,128)(2,1)S(1)}, u32[]{:S(2)}, u32[]{:S(2)}) collective-permute-start(bf16[16,1280]{1,0:T(8,128)(2,1)S(1)} %shard_map.42), channel_id=1, source_target_pairs={{0,12},{1,13},{2,14},{3,15},{4,8},{5,9},{6,10},{7,11},{8,4},{9,5},... | collective-permute-start | bytes 122888 | tf_op jit(solution)/shard_map/ppermute | solution.py:25
  7.4 4.9 %collective-permute-start.2 = (bf16[16,1280]{1,0:T(8,128)(2,1)S(1)}, bf16[16,1280]{1,0:T(8,128)(2,1)S(1)}, u32[]{:S(2)}, u32[]{:S(2)}) collective-permute-start(bf16[16,1280]{1,0:T(8,128)(2,1)S(1)} %shard_map.42), channel_id=1, source_target_pairs={{0,8},{1,9},{2,10},{3,11},{4,12},{5,13},{6,14},{7,15},{8,0},{9,1},... | collective-permute-start | bytes 122888 | tf_op jit(solution)/shard_map/ppermute | solution.py:25
  7.4 4.9 %collective-permute-start.3 = (bf16[16,1280]{1,0:T(8,128)(2,1)S(1)}, bf16[16,1280]{1,0:T(8,128)(2,1)S(1)}, u32[]{:S(2)}, u32[]{:S(2)}) collective-permute-start(bf16[16,1280]{1,0:T(8,128)(2,1)S(1)} %shard_map.42), channel_id=1, source_target_pairs={{0,4},{1,5},{2,6},{3,7},{4,0},{5,1},{6,2},{7,3},{8,12},{9,13},{10,... | collective-permute-start | bytes 122888 | tf_op jit(solution)/shard_map/ppermute | solution.py:25
  12.4 5.5 %collective-permute-start.5 = (bf16[64,1280]{1,0:T(8,128)(2,1)S(1)}, bf16[64,1280]{1,0:T(8,128)(2,1)S(1)}, u32[]{:S(2)}, u32[]{:S(2)}) collective-permute-start(bf16[64,1280]{1,0:T(8,128)(2,1)S(1)} %pad_maximum_fusion.2), channel_id=1, source_target_pairs={{0,2},{1,3},{2,0},{3,1},{4,6},{5,7},{6,4},{7,5},{8,10},{9,11},{10,... | collective-permute-start | bytes 491528 | tf_op jit(solution)/shard_map/ppermute | solution.py:25
  14.6 5.8 %collective-permute-start.7 = (bf16[64,1280]{1,0:T(8,128)(2,1)S(1)}, bf16[64,1280]{1,0:T(8,128)(2,1)S(1)}, u32[]{:S(2)}, u32[]{:S(2)}) collective-permute-start(bf16[64,1280]{1,0:T(8,128)(2,1)S(1)} %pad_maximum_fusion.2), channel_id=1, source_target_pairs={{0,16},{16,0},{1,17},{17,1},{2,18},{18,2},{3,19},{19,3},{4,20},{20... | collective-permute-start | bytes 491528 | tf_op jit(solution)/shard_map/ppermute | solution.py:206
  18.9 4.0 %collective-permute-start.6 = (f32[72,128]{1,0:T(8,128)S(1)}, f32[72,128]{1,0:T(8,128)S(1)}, u32[]{:S(2)}, u32[]{:S(2)}) collective-permute-start(f32[72,128]{1,0:T(8,128)S(1)} %get-tuple-element.54), channel_id=1, source_target_pairs={{0,2},{1,3},{2,0},{3,1},{4,6},{5,7},{6,4},{7,5},{8,10},{9,11},{10,... | collective-permute-start | bytes 110600 | tf_op jit(solution)/shard_map/ppermute | solution.py:25
  22.9 6.3 %collective-permute-start.11 = (bf16[128,1280]{1,0:T(8,128)(2,1)S(1)}, bf16[128,1280]{1,0:T(8,128)(2,1)S(1)}, u32[]{:S(2)}, u32[]{:S(2)}) collective-permute-start(bf16[128,1280]{1,0:T(8,128)(2,1)S(1)} %pad_maximum_fusion.1.refs_0_), channel_id=1, source_target_pairs={{0,1},{1,0},{2,3},{3,2},{4,5},{5,4},{6,7},{7,6},{8,9},{9,8},{10,11... | collective-permute-start | bytes 983048 | tf_op jit(solution)/shard_map/ppermute | solution.py:25
  22.9 6.8 %collective-permute-start.8 = (f32[72,128]{1,0:T(8,128)S(1)}, f32[72,128]{1,0:T(8,128)S(1)}, u32[]{:S(2)}, u32[]{:S(2)}) collective-permute-start(f32[72,128]{1,0:T(8,128)S(1)} %add.24), channel_id=1, source_target_pairs={{0,12},{1,13},{2,14},{3,15},{4,8},{5,9},{6,10},{7,11},{8,4},{9,5},... | collective-permute-start | bytes 110600 | tf_op jit(solution)/shard_map/ppermute | solution.py:25
  25.2 5.1 %collective-permute-start.9 = (f32[72,128]{1,0:T(8,128)S(1)}, f32[72,128]{1,0:T(8,128)S(1)}, u32[]{:S(2)}, u32[]{:S(2)}) collective-permute-start(f32[72,128]{1,0:T(8,128)S(1)} %add.24), channel_id=1, source_target_pairs={{0,8},{1,9},{2,10},{3,11},{4,12},{5,13},{6,14},{7,15},{8,0},{9,1},... | collective-permute-start | bytes 110600 | tf_op jit(solution)/shard_map/ppermute | solution.py:25
  25.2 5.1 %collective-permute-start.10 = (f32[72,128]{1,0:T(8,128)S(1)}, f32[72,128]{1,0:T(8,128)S(1)}, u32[]{:S(2)}, u32[]{:S(2)}) collective-permute-start(f32[72,128]{1,0:T(8,128)S(1)} %add.24), channel_id=1, source_target_pairs={{0,4},{1,5},{2,6},{3,7},{4,0},{5,1},{6,2},{7,3},{8,12},{9,13},{10,... | collective-permute-start | bytes 110600 | tf_op jit(solution)/shard_map/ppermute | solution.py:25
  27.6 9.7 %collective-permute-start.13 = (bf16[64,1280]{1,0:T(8,128)(2,1)S(1)}, bf16[64,1280]{1,0:T(8,128)(2,1)S(1)}, u32[]{:S(2)}, u32[]{:S(2)}) collective-permute-start(bf16[64,1280]{1,0:T(8,128)(2,1)S(1)} %collective-permute-done.5), channel_id=1, source_target_pairs={{0,16},{16,0},{1,17},{17,1},{2,18},{18,2},{3,19},{19,3},{4,20},{20... | collective-permute-start | bytes 491528 | tf_op jit(solution)/shard_map/ppermute | solution.py:206
  31.1 6.1 %collective-permute-start.12 = (bf16[64,1280]{1,0:T(8,128)(2,1)S(1)}, bf16[64,1280]{1,0:T(8,128)(2,1)S(1)}, u32[]{:S(2)}, u32[]{:S(2)}) collective-permute-start(bf16[64,1280]{1,0:T(8,128)(2,1)S(1)} %get-tuple-element.70), channel_id=1, source_target_pairs={{0,2},{1,3},{2,0},{3,1},{4,6},{5,7},{6,4},{7,5},{8,10},{9,11},{10,... | collective-permute-start | bytes 491528 | tf_op jit(solution)/shard_map/ppermute | solution.py:25
  33.5 1.7 %collective-permute-start.19 = (bf16[128,512]{1,0:T(8,128)(2,1)S(1)}, bf16[128,512]{1,0:T(8,128)(2,1)S(1)}, u32[]{:S(2)}, u32[]{:S(2)}) collective-permute-start(bf16[128,512]{1,0:T(8,128)(2,1)S(1)} %slice.42), channel_id=1, source_target_pairs={{0,1},{1,0},{2,3},{3,2},{4,5},{5,4},{6,7},{7,6},{8,9},{9,8},{10,11... | collective-permute-start | bytes 393224 | tf_op jit(solution)/shard_map/ppermute | solution.py:25
  33.6 6.4 %collective-permute-start.18 = (bf16[128,512]{1,0:T(8,128)(2,1)S(1)}, bf16[128,512]{1,0:T(8,128)(2,1)S(1)}, u32[]{:S(2)}, u32[]{:S(2)}) collective-permute-start(bf16[128,512]{1,0:T(8,128)(2,1)S(1)} %slice.35.refs_2_), channel_id=1, source_target_pairs={{0,16},{16,0},{1,17},{17,1},{2,18},{18,2},{3,19},{19,3},{4,20},{20... | collective-permute-start | bytes 393224 | tf_op jit(solution)/shard_map/ppermute | solution.py:206
  35.2 7.2 %collective-permute-start.20 = (bf16[128,512]{1,0:T(8,128)(2,1)S(1)}, bf16[128,512]{1,0:T(8,128)(2,1)S(1)}, u32[]{:S(2)}, u32[]{:S(2)}) collective-permute-start(bf16[128,512]{1,0:T(8,128)(2,1)S(1)} %collective-permute-done.19.refs_3_), channel_id=1, source_target_pairs={{0,16},{16,0},{1,17},{17,1},{2,18},{18,2},{3,19},{19,3},{4,20},{20... | collective-permute-start | bytes 393224 | tf_op jit(solution)/shard_map/ppermute | solution.py:206
  37.3 5.6 %collective-permute-start.17 = (bf16[128,1280]{1,0:T(8,128)(2,1)S(1)}, bf16[128,1280]{1,0:T(8,128)(2,1)S(1)}, u32[]{:S(2)}, u32[]{:S(2)}) collective-permute-start(bf16[128,1280]{1,0:T(8,128)(2,1)S(1)} %constant_dynamic-update-slice_fusion.2.refs_0_), channel_id=1, source_target_pairs={{0,1},{1,0},{2,3},{3,2},{4,5},{5,4},{6,7},{7,6},{8,9},{9,8},{10,11... | collective-permute-start | bytes 983048 | tf_op jit(solution)/shard_map/ppermute | solution.py:25
  37.4 7.3 %collective-permute-start.14 = (bf16[16,1280]{1,0:T(8,128)(2,1)S(1)}, bf16[16,1280]{1,0:T(8,128)(2,1)S(1)}, u32[]{:S(2)}, u32[]{:S(2)}) collective-permute-start(bf16[16,1280]{1,0:T(8,128)(2,1)S(1)} %get-tuple-element.90), channel_id=1, source_target_pairs={{0,12},{1,13},{2,14},{3,15},{4,8},{5,9},{6,10},{7,11},{8,4},{9,5},... | collective-permute-start | bytes 122888 | tf_op jit(solution)/shard_map/ppermute | solution.py:25
  39.7 5.3 %collective-permute-start.15 = (bf16[16,1280]{1,0:T(8,128)(2,1)S(1)}, bf16[16,1280]{1,0:T(8,128)(2,1)S(1)}, u32[]{:S(2)}, u32[]{:S(2)}) collective-permute-start(bf16[16,1280]{1,0:T(8,128)(2,1)S(1)} %get-tuple-element.89), channel_id=1, source_target_pairs={{0,8},{1,9},{2,10},{3,11},{4,12},{5,13},{6,14},{7,15},{8,0},{9,1},... | collective-permute-start | bytes 122888 | tf_op jit(solution)/shard_map/ppermute | solution.py:25
  40.0 5.0 %collective-permute-start.16 = (bf16[16,1280]{1,0:T(8,128)(2,1)S(1)}, bf16[16,1280]{1,0:T(8,128)(2,1)S(1)}, u32[]{:S(2)}, u32[]{:S(2)}) collective-permute-start(bf16[16,1280]{1,0:T(8,128)(2,1)S(1)} %get-tuple-element.88), channel_id=1, source_target_pairs={{0,4},{1,5},{2,6},{3,7},{4,0},{5,1},{6,2},{7,3},{8,12},{9,13},{10,... | collective-permute-start | bytes 122888 | tf_op jit(solution)/shard_map/ppermute | solution.py:25
  45.0 1.3 %collective-permute-start.21 = (f32[8,1280]{1,0:T(8,128)S(1)}, f32[8,1280]{1,0:T(8,128)S(1)}, u32[]{:S(2)}, u32[]{:S(2)}) collective-permute-start(f32[8,1280]{1,0:T(8,128)S(1)} %get-tuple-element.91), channel_id=1, source_target_pairs={{0,1},{1,0},{2,3},{3,2},{4,5},{5,4},{6,7},{7,6},{8,9},{9,8},{10,11... | collective-permute-start | bytes 122888 | tf_op jit(solution)/shard_map/ppermute | solution.py:25

commit v3 on v1

--- a/solution.py
+++ b/solution.py
@@ -289,7 +289,7 @@
         (grad, grad_others, grad_core_others)
     )
     weight_grad = weight_part(rows, rows_core, grad, grad_core)
-    height = min(depth, 256)
+    height = min(depth, 128)
     for left, (theirs, theirs_grad) in enumerate(zip(rows_others, grad_others), 2 - groups):
         operands = [
             theirs, swap(theirs, "dp", CORE),

time: 47.1 us -> 47.1 us (level)
  no operation moved by 1% of the time
where the time goes in v3:
time: 47.1 us; the launch traced here: 46.9 us
  starting transfers between devices  24.5 us (52%)
  waiting for transfers between devices  11.2 us (24%)
  Pallas kernels  5.95 us (13%)
  other arithmetic  1.8 us (4%)
  matrix products  1.68 us (4%)
  between operations  0.88 us (2%)
  local copies, waits for them, and re-layouts  0.86 us (2%)
    ppermute x18, starting transfers between devices, swap(): lax.ppermute(block, axis, [(i, i ^ bits) for i in range(lax.axis_size(axi...  18.6 us
    ppermute x18, waiting for transfers between devices, swap(): lax.ppermute(block, axis, [(i, i ^ bits) for i in range(lax.axis_size(axi...  11 us
    ppermute x4, starting transfers between devices, over_rep(): lax.ppermute(array, 'rep', [(i, (i + shift) % groups) for i in range(grou...  5.98 us
    pallas_call x1, Pallas kernels, shards(): call(last_weight_kernel, struct((depth, block), F32), [VMEM] * 5, [pltpu....  1.79 us
    dot_general x3, matrix products, matmul(): return jnp.dot(rows, matrix, preferred_element_type=F32)  1.68 us
    concatenate x1, other arithmetic, shards(): wide = jnp.concatenate([weight, weight_core], axis=1)  1.67 us
    pallas_call x2, Pallas kernels, grads(): call(functools.partial(grads_kernel, side, scale, features), (struct((hal...  1.57 us
  transfers between devices with their start and end apart: 22, of which 11 were waited for; matrix products, arithmetic and copies ran while one was open for 7% of the time, Pallas kernels for 11%

profile of v3, /device:TPU:0, one launch (start us, length us, event | category | flops | bytes accessed | tf_op | source)
XLA Modules:
  0.0 46.9 jit_solution(2320560340561987859)
XLA Ops:
  1.1 0.8 %copy-done = bf16[8,2,1280]{2,1,0:T(2,128)(2,1)S(1)} copy-done((bf16[8,2,1280]{2,1,0:T(2,128)(2,1)S(1)}, bf16[8,2,1280]{2,1,0:T(2,128)(2,1)}, u32[]{:S(2)}) %copy-start) | copy-done | bytes 40984
  2.6 4.8 %collective-permute-start.1 = (bf16[16,1280]{1,0:T(8,128)(2,1)S(1)}, bf16[16,1280]{1,0:T(8,128)(2,1)S(1)}, u32[]{:S(2)}, u32[]{:S(2)}) collective-permute-start(bf16[16,1280]{1,0:T(8,128)(2,1)S(1)} %shard_map.42), channel_id=1, source_target_pairs={{0,12},{1,13},{2,14},{3,15},{4,8},{5,9},{6,10},{7,11},{8,4},{9,5},... | collective-permute-start | bytes 122888 | tf_op jit(solution)/shard_map/ppermute | solution.py:25
  7.4 0.6 %collective-permute-start.3 = (bf16[16,1280]{1,0:T(8,128)(2,1)S(1)}, bf16[16,1280]{1,0:T(8,128)(2,1)S(1)}, u32[]{:S(2)}, u32[]{:S(2)}) collective-permute-start(bf16[16,1280]{1,0:T(8,128)(2,1)S(1)} %shard_map.42), channel_id=1, source_target_pairs={{0,4},{1,5},{2,6},{3,7},{4,0},{5,1},{6,2},{7,3},{8,12},{9,13},{10,... | collective-permute-start | bytes 122888 | tf_op jit(solution)/shard_map/ppermute | solution.py:25
  8.1 1.7 %pad_maximum_fusion.wide_ref = bf16[1280,1024]{1,0:T(8,128)(2,1)S(1)} fusion(bf16[1280,512]{1,0:T(8,128)(2,1)S(1)} %collective-permute-done.4, bf16[1280,512]{1,0:T(8,128)(2,1)} %param.3), kind=kLoop, calls=%fused_computation | loop fusion | flops 5242880 | bytes 5242880 | tf_op jit(solution)/shard_map/concatenate | solution.py:219
  9.8 2.6 %collective-permute-done.2 = bf16[16,1280]{1,0:T(8,128)(2,1)S(1)} collective-permute-done((bf16[16,1280]{1,0:T(8,128)(2,1)S(1)}, bf16[16,1280]{1,0:T(8,128)(2,1)S(1)}, u32[]{:S(2)}, u32[]{:S(2)}) %collective-permute-start.2) | collective-permute-done | bytes 40992 | tf_op jit(solution)/shard_map/ppermute | solution.py:25
  12.4 1.6 %collective-permute-start.5 = (bf16[64,1280]{1,0:T(8,128)(2,1)S(1)}, bf16[64,1280]{1,0:T(8,128)(2,1)S(1)}, u32[]{:S(2)}, u32[]{:S(2)}) collective-permute-start(bf16[64,1280]{1,0:T(8,128)(2,1)S(1)} %pad_maximum_fusion.2), channel_id=1, source_target_pairs={{0,2},{1,3},{2,0},{3,1},{4,6},{5,7},{6,4},{7,5},{8,10},{9,11},{10,... | collective-permute-start | bytes 491528 | tf_op jit(solution)/shard_map/ppermute | solution.py:25
  13.9 0.7 %shard_map.44.w_ref = bf16[1024,1280]{1,0:T(8,128)(2,1)S(1)} custom-call(bf16[1280,1024]{1,0:T(8,128)(2,1)S(1)} %pad_maximum_fusion.wide_ref), custom_call_target="tpu_custom_call" | custom-call | tf_op jit(solution)/shard_map/pallas_call | solution.py:225
  14.6 1.6 %collective-permute-start.9 = (bf16[64,1280]{1,0:T(8,128)(2,1)S(1)}, bf16[64,1280]{1,0:T(8,128)(2,1)S(1)}, u32[]{:S(2)}, u32[]{:S(2)}) collective-permute-start(bf16[64,1280]{1,0:T(8,128)(2,1)S(1)} %pad_maximum_fusion.2), channel_id=1, source_target_pairs={{0,16},{16,0},{1,17},{17,1},{2,18},{18,2},{3,19},{19,3},{4,20},{20... | collective-permute-start | bytes 491528 | tf_op jit(solution)/shard_map/ppermute | solution.py:206
  16.2 0.6 %fusion.2.near_ref.z_ref = f32[64,1024]{1,0:T(8,128)S(1)} fusion(bf16[64,1280]{1,0:T(8,128)(2,1)S(1)} %pad_maximum_fusion.2, bf16[1280,1024]{1,0:T(8,128)(2,1)S(1)} %pad_maximum_fusion.wide_ref), kind=kOutput, calls=%fused_computation.12 | convolution fusion | flops 167772160 | bytes 3047424 | tf_op jit(solution)/shard_map/dot_general | solution.py:211
  16.8 1.1 %collective-permute-done.5 = bf16[64,1280]{1,0:T(8,128)(2,1)S(1)} collective-permute-done((bf16[64,1280]{1,0:T(8,128)(2,1)S(1)}, bf16[64,1280]{1,0:T(8,128)(2,1)S(1)}, u32[]{:S(2)}, u32[]{:S(2)}) %collective-permute-start.5) | collective-permute-done | bytes 163872 | tf_op jit(solution)/shard_map/ppermute | solution.py:25
  17.9 0.6 %fusion.3.far_ref.z_ref = f32[64,1024]{1,0:T(8,128)S(1)} fusion(bf16[64,1280]{1,0:T(8,128)(2,1)S(1)} %collective-permute-done.5, bf16[1280,1024]{1,0:T(8,128)(2,1)S(1)} %pad_maximum_fusion.wide_ref), kind=kOutput, calls=%fused_computation.13 | convolution fusion | flops 167772160 | bytes 3047424 | tf_op jit(solution)/shard_map/dot_general | solution.py:211
  18.9 2.9 %collective-permute-start.6 = (f32[72,128]{1,0:T(8,128)S(1)}, f32[72,128]{1,0:T(8,128)S(1)}, u32[]{:S(2)}, u32[]{:S(2)}) collective-permute-start(f32[72,128]{1,0:T(8,128)S(1)} %get-tuple-element.55), channel_id=1, source_target_pairs={{0,10},{1,11},{2,8},{3,9},{4,14},{5,15},{6,12},{7,13},{8,2},{9,3},... | collective-permute-start | bytes 110600 | tf_op jit(solution)/shard_map/ppermute | solution.py:25
  21.7 1.0 %collective-permute-start.7 = (f32[72,128]{1,0:T(8,128)S(1)}, f32[72,128]{1,0:T(8,128)S(1)}, u32[]{:S(2)}, u32[]{:S(2)}) collective-permute-start(f32[72,128]{1,0:T(8,128)S(1)} %get-tuple-element.55), channel_id=1, source_target_pairs={{0,8},{1,9},{2,10},{3,11},{4,12},{5,13},{6,14},{7,15},{8,0},{9,1},... | collective-permute-start | bytes 110600 | tf_op jit(solution)/shard_map/ppermute | solution.py:25
  22.8 0.5 %collective-permute-start.8 = (f32[72,128]{1,0:T(8,128)S(1)}, f32[72,128]{1,0:T(8,128)S(1)}, u32[]{:S(2)}, u32[]{:S(2)}) collective-permute-start(f32[72,128]{1,0:T(8,128)S(1)} %get-tuple-element.55), channel_id=1, source_target_pairs={{0,2},{1,3},{2,0},{3,1},{4,6},{5,7},{6,4},{7,5},{8,10},{9,11},{10,... | collective-permute-start | bytes 110600 | tf_op jit(solution)/shard_map/ppermute | solution.py:25
  23.3 2.0 %collective-permute-done.6 = f32[72,128]{1,0:T(8,128)S(1)} collective-permute-done((f32[72,128]{1,0:T(8,128)S(1)}, f32[72,128]{1,0:T(8,128)S(1)}, u32[]{:S(2)}, u32[]{:S(2)}) %collective-permute-start.6) | collective-permute-done | bytes 36896 | tf_op jit(solution)/shard_map/ppermute | solution.py:25
  25.3 1.3 %collective-permute-done.7 = f32[72,128]{1,0:T(8,128)S(1)} collective-permute-done((f32[72,128]{1,0:T(8,128)S(1)}, f32[72,128]{1,0:T(8,128)S(1)}, u32[]{:S(2)}, u32[]{:S(2)}) %collective-permute-start.7) | collective-permute-done | bytes 36896 | tf_op jit(solution)/shard_map/ppermute | solution.py:25
  26.8 0.9 %collective-permute-start.10 = (f32[72,128]{1,0:T(8,128)S(1)}, f32[72,128]{1,0:T(8,128)S(1)}, u32[]{:S(2)}, u32[]{:S(2)}) collective-permute-start(f32[72,128]{1,0:T(8,128)S(1)} %add_add_fusion), channel_id=1, source_target_pairs={{0,4},{1,5},{2,6},{3,7},{4,0},{5,1},{6,2},{7,3},{8,12},{9,13},{10,... | collective-permute-start | bytes 110600 | tf_op jit(solution)/shard_map/ppermute | solution.py:25
  27.9 1.6 %collective-permute-start.13 = (bf16[64,1280]{1,0:T(8,128)(2,1)S(1)}, bf16[64,1280]{1,0:T(8,128)(2,1)S(1)}, u32[]{:S(2)}, u32[]{:S(2)}) collective-permute-start(bf16[64,1280]{1,0:T(8,128)(2,1)S(1)} %collective-permute-done.5), channel_id=1, source_target_pairs={{0,16},{16,0},{1,17},{17,1},{2,18},{18,2},{3,19},{19,3},{4,20},{20... | collective-permute-start | bytes 491528 | tf_op jit(solution)/shard_map/ppermute | solution.py:206
  30.1 0.8 %collective-permute-done.10 = f32[72,128]{1,0:T(8,128)S(1)} collective-permute-done((f32[72,128]{1,0:T(8,128)S(1)}, f32[72,128]{1,0:T(8,128)S(1)}, u32[]{:S(2)}, u32[]{:S(2)}) %collective-permute-start.10) | collective-permute-done | bytes 36896 | tf_op jit(solution)/shard_map/ppermute | solution.py:25
  30.9 0.8 %shard_map.46 = (bf16[64,1024]{1,0:T(8,128)(2,1)S(1)}, bf16[64,1280]{1,0:T(8,128)(2,1)S(1)}) custom-call(s32[1]{0:T(128)} %bitcast.me_ref, f32[72,128]{1,0:T(8,128)S(1)} %add.27.packed_ref, bf16[128,1024]{1,0:T(8,128)(2,1)S(1)} %get-tuple-element.68.c_ref, f32[64,1024]{1,0:T(8,128)S(1)} %fusion.3.far_ref.z_ref, f32[128,1024]{1,0:T(8,128)S(1)} %fusion.4.other_ref, ...), custom_call_target="tpu_custom_call" | custom-call | tf_op jit(solution)/shard_map/pallas_call | solution.py:261
  31.6 0.6 %collective-permute-start.12 = (bf16[64,1280]{1,0:T(8,128)(2,1)S(1)}, bf16[64,1280]{1,0:T(8,128)(2,1)S(1)}, u32[]{:S(2)}, u32[]{:S(2)}) collective-permute-start(bf16[64,1280]{1,0:T(8,128)(2,1)S(1)} %get-tuple-element.72), channel_id=1, source_target_pairs={{0,2},{1,3},{2,0},{3,1},{4,6},{5,7},{6,4},{7,5},{8,10},{9,11},{10,... | collective-permute-start | bytes 491528 | tf_op jit(solution)/shard_map/ppermute | solution.py:25
  32.3 0.8 %shard_map.47 = (bf16[64,1024]{1,0:T(8,128)(2,1)S(1)}, f32[64,1280]{1,0:T(8,128)S(1)}) custom-call(s32[1]{0:T(128)} %bitcast.me_ref, f32[72,128]{1,0:T(8,128)S(1)} %add.27.packed_ref, bf16[128,1024]{1,0:T(8,128)(2,1)S(1)} %get-tuple-element.68.c_ref, f32[64,1024]{1,0:T(8,128)S(1)} %fusion.2.near_ref.z_ref, f32[128,1024]{1,0:T(8,128)S(1)} %fusion.4.other_ref, ...), custom_call_target="tpu_custom_call" | custom-call | tf_op jit(solution)/shard_map/pallas_call | solution.py:261
  33.2 1.6 %collective-permute-start.18 = (bf16[128,512]{1,0:T(8,128)(2,1)S(1)}, bf16[128,512]{1,0:T(8,128)(2,1)S(1)}, u32[]{:S(2)}, u32[]{:S(2)}) collective-permute-start(bf16[128,512]{1,0:T(8,128)(2,1)S(1)} %slice.35.refs_2_), channel_id=1, source_target_pairs={{0,16},{16,0},{1,17},{17,1},{2,18},{18,2},{3,19},{19,3},{4,20},{20... | collective-permute-start | bytes 393224 | tf_op jit(solution)/shard_map/ppermute | solution.py:206
  34.8 1.2 %collective-permute-start.20 = (bf16[128,512]{1,0:T(8,128)(2,1)S(1)}, bf16[128,512]{1,0:T(8,128)(2,1)S(1)}, u32[]{:S(2)}, u32[]{:S(2)}) collective-permute-start(bf16[128,512]{1,0:T(8,128)(2,1)S(1)} %collective-permute-done.19.refs_3_), channel_id=1, source_target_pairs={{0,16},{16,0},{1,17},{17,1},{2,18},{18,2},{3,19},{19,3},{4,20},{20... | collective-permute-start | bytes 393224 | tf_op jit(solution)/shard_map/ppermute | solution.py:206
  36.0 1.1 %collective-permute-done.12 = bf16[64,1280]{1,0:T(8,128)(2,1)S(1)} collective-permute-done((bf16[64,1280]{1,0:T(8,128)(2,1)S(1)}, bf16[64,1280]{1,0:T(8,128)(2,1)S(1)}, u32[]{:S(2)}, u32[]{:S(2)}) %collective-permute-start.12) | collective-permute-done | bytes 163872 | tf_op jit(solution)/shard_map/ppermute | solution.py:25
  37.3 2.4 %collective-permute-start.14 = (bf16[16,1280]{1,0:T(8,128)(2,1)S(1)}, bf16[16,1280]{1,0:T(8,128)(2,1)S(1)}, u32[]{:S(2)}, u32[]{:S(2)}) collective-permute-start(bf16[16,1280]{1,0:T(8,128)(2,1)S(1)} %get-tuple-element.92), channel_id=1, source_target_pairs={{0,12},{1,13},{2,14},{3,15},{4,8},{5,9},{6,10},{7,11},{8,4},{9,5},... | collective-permute-start | bytes 122888 | tf_op jit(solution)/shard_map/ppermute | solution.py:25
  39.9 1.9 %collective-permute-start.16 = (bf16[16,1280]{1,0:T(8,128)(2,1)S(1)}, bf16[16,1280]{1,0:T(8,128)(2,1)S(1)}, u32[]{:S(2)}, u32[]{:S(2)}) collective-permute-start(bf16[16,1280]{1,0:T(8,128)(2,1)S(1)} %get-tuple-element.90), channel_id=1, source_target_pairs={{0,4},{1,5},{2,6},{3,7},{4,0},{5,1},{6,2},{7,3},{8,12},{9,13},{10,... | collective-permute-start | bytes 122888 | tf_op jit(solution)/shard_map/ppermute | solution.py:25
  42.0 0.5 %shard_map.48.refs_4_ = f32[1280,512]{1,0:T(8,128)S(1)} custom-call(bf16[128,1280]{1,0:T(8,128)(2,1)S(1)} %pad_maximum_fusion.1.refs_0_, bf16[128,1280]{1,0:T(8,128)(2,1)S(1)} %collective-permute-done.11.refs_1_, bf16[128,512]{1,0:T(8,128)(2,1)S(1)} %slice.35.refs_2_, bf16[128,512]{1,0:T(8,128)(2,1)S(1)} %collective-permute-done.19.refs_3_), custom_call_target="tpu_custom_call" | custom-call | tf_op jit(solution)/shard_map/pallas_call | solution.py:271
  42.5 1.8 %shard_map.49 = f32[1280,512]{1,0:T(8,128)} custom-call(bf16[128,1280]{1,0:T(8,128)(2,1)S(1)} %constant_dynamic-update-slice_fusion.2.refs_0_, bf16[128,1280]{1,0:T(8,128)(2,1)S(1)} %collective-permute-done.17.refs_1_, bf16[128,512]{1,0:T(8,128)(2,1)S(1)} %collective-permute-done.18.refs_2_, bf16[128,512]{1,0:T(8,128)(2,1)S(1)} %collective-permute-done.20.refs_3_, ...), custom_call_target="tpu_custom_call" | custom-call | tf_op jit(solution)/shard_map/pallas_call | solution.py:301
  44.3 0.6 %collective-permute-done.15 = bf16[16,1280]{1,0:T(8,128)(2,1)S(1)} collective-permute-done((bf16[16,1280]{1,0:T(8,128)(2,1)S(1)}, bf16[16,1280]{1,0:T(8,128)(2,1)S(1)}, u32[]{:S(2)}, u32[]{:S(2)}) %collective-permute-start.15) | collective-permute-done | bytes 40992 | tf_op jit(solution)/shard_map/ppermute | solution.py:25
  45.1 1.2 %collective-permute-done.21.other_ref = f32[8,1280]{1,0:T(8,128)S(1)} collective-permute-done((f32[8,1280]{1,0:T(8,128)S(1)}, f32[8,1280]{1,0:T(8,128)S(1)}, u32[]{:S(2)}, u32[]{:S(2)}) %collective-permute-start.21) | collective-permute-done | bytes 40992 | tf_op jit(solution)/shard_map/ppermute | solution.py:25
  46.3 0.7 %shard_map.50 = f32[8,2,1280]{2,1,0:T(2,128)} custom-call(s32[1]{0:T(128)} %bitcast.me_ref, f32[8,1280]{1,0:T(8,128)S(1)} %get-tuple-element.94.own_ref, f32[8,1280]{1,0:T(8,128)S(1)} %collective-permute-done.21.other_ref), custom_call_target="tpu_custom_call" | custom-call | tf_op jit(solution)/shard_map/pallas_call | solution.py:314
  (43 shorter events, 3.4 us)
Async XLA Ops:
  0.6 1.6 %collective-permute-start = (bf16[8,2,1280]{2,1,0:T(2,128)(2,1)}, bf16[8,2,1280]{2,1,0:T(2,128)(2,1)S(1)}, u32[]{:S(2)}, u32[]{:S(2)}) collective-permute-start(bf16[8,2,1280]{2,1,0:T(2,128)(2,1)} %images_ref.1), channel_id=1, source_target_pairs={{0,1},{1,0},{2,3},{3,2},{4,5},{5,4},{6,7},{7,6},{8,9},{9,8},{10,11... | collective-permute-start | bytes 122888 | tf_op jit(solution)/shard_map/ppermute | solution.py:25
  1.1 0.8 %copy-start = (bf16[8,2,1280]{2,1,0:T(2,128)(2,1)S(1)}, bf16[8,2,1280]{2,1,0:T(2,128)(2,1)}, u32[]{:S(2)}) copy-start(bf16[8,2,1280]{2,1,0:T(2,128)(2,1)} %images_ref.1) | copy-start | bytes 122884
  2.2 5.9 %collective-permute-start.4 = (bf16[1280,512]{1,0:T(8,128)(2,1)}, bf16[1280,512]{1,0:T(8,128)(2,1)S(1)}, u32[]{:S(2)}, u32[]{:S(2)}) collective-permute-start(bf16[1280,512]{1,0:T(8,128)(2,1)} %param.3), channel_id=1, source_target_pairs={{0,1},{1,0},{2,3},{3,2},{4,5},{5,4},{6,7},{7,6},{8,9},{9,8},{10,11... | collective-permute-start | bytes 3932168 | tf_op jit(solution)/shard_map/ppermute | solution.py:25
  2.6 7.2 %collective-permute-start.1 = (bf16[16,1280]{1,0:T(8,128)(2,1)S(1)}, bf16[16,1280]{1,0:T(8,128)(2,1)S(1)}, u32[]{:S(2)}, u32[]{:S(2)}) collective-permute-start(bf16[16,1280]{1,0:T(8,128)(2,1)S(1)} %shard_map.42), channel_id=1, source_target_pairs={{0,12},{1,13},{2,14},{3,15},{4,8},{5,9},{6,10},{7,11},{8,4},{9,5},... | collective-permute-start | bytes 122888 | tf_op jit(solution)/shard_map/ppermute | solution.py:25
  7.4 4.9 %collective-permute-start.2 = (bf16[16,1280]{1,0:T(8,128)(2,1)S(1)}, bf16[16,1280]{1,0:T(8,128)(2,1)S(1)}, u32[]{:S(2)}, u32[]{:S(2)}) collective-permute-start(bf16[16,1280]{1,0:T(8,128)(2,1)S(1)} %shard_map.42), channel_id=1, source_target_pairs={{0,8},{1,9},{2,10},{3,11},{4,12},{5,13},{6,14},{7,15},{8,0},{9,1},... | collective-permute-start | bytes 122888 | tf_op jit(solution)/shard_map/ppermute | solution.py:25
  7.4 4.9 %collective-permute-start.3 = (bf16[16,1280]{1,0:T(8,128)(2,1)S(1)}, bf16[16,1280]{1,0:T(8,128)(2,1)S(1)}, u32[]{:S(2)}, u32[]{:S(2)}) collective-permute-start(bf16[16,1280]{1,0:T(8,128)(2,1)S(1)} %shard_map.42), channel_id=1, source_target_pairs={{0,4},{1,5},{2,6},{3,7},{4,0},{5,1},{6,2},{7,3},{8,12},{9,13},{10,... | collective-permute-start | bytes 122888 | tf_op jit(solution)/shard_map/ppermute | solution.py:25
  12.4 5.5 %collective-permute-start.5 = (bf16[64,1280]{1,0:T(8,128)(2,1)S(1)}, bf16[64,1280]{1,0:T(8,128)(2,1)S(1)}, u32[]{:S(2)}, u32[]{:S(2)}) collective-permute-start(bf16[64,1280]{1,0:T(8,128)(2,1)S(1)} %pad_maximum_fusion.2), channel_id=1, source_target_pairs={{0,2},{1,3},{2,0},{3,1},{4,6},{5,7},{6,4},{7,5},{8,10},{9,11},{10,... | collective-permute-start | bytes 491528 | tf_op jit(solution)/shard_map/ppermute | solution.py:25
  14.6 12.1 %collective-permute-start.9 = (bf16[64,1280]{1,0:T(8,128)(2,1)S(1)}, bf16[64,1280]{1,0:T(8,128)(2,1)S(1)}, u32[]{:S(2)}, u32[]{:S(2)}) collective-permute-start(bf16[64,1280]{1,0:T(8,128)(2,1)S(1)} %pad_maximum_fusion.2), channel_id=1, source_target_pairs={{0,16},{16,0},{1,17},{17,1},{2,18},{18,2},{3,19},{19,3},{4,20},{20... | collective-permute-start | bytes 491528 | tf_op jit(solution)/shard_map/ppermute | solution.py:206
  18.9 6.4 %collective-permute-start.6 = (f32[72,128]{1,0:T(8,128)S(1)}, f32[72,128]{1,0:T(8,128)S(1)}, u32[]{:S(2)}, u32[]{:S(2)}) collective-permute-start(f32[72,128]{1,0:T(8,128)S(1)} %get-tuple-element.55), channel_id=1, source_target_pairs={{0,10},{1,11},{2,8},{3,9},{4,14},{5,15},{6,12},{7,13},{8,2},{9,3},... | collective-permute-start | bytes 110600 | tf_op jit(solution)/shard_map/ppermute | solution.py:25
  21.7 4.9 %collective-permute-start.7 = (f32[72,128]{1,0:T(8,128)S(1)}, f32[72,128]{1,0:T(8,128)S(1)}, u32[]{:S(2)}, u32[]{:S(2)}) collective-permute-start(f32[72,128]{1,0:T(8,128)S(1)} %get-tuple-element.55), channel_id=1, source_target_pairs={{0,8},{1,9},{2,10},{3,11},{4,12},{5,13},{6,14},{7,15},{8,0},{9,1},... | collective-permute-start | bytes 110600 | tf_op jit(solution)/shard_map/ppermute | solution.py:25
  22.8 4.0 %collective-permute-start.8 = (f32[72,128]{1,0:T(8,128)S(1)}, f32[72,128]{1,0:T(8,128)S(1)}, u32[]{:S(2)}, u32[]{:S(2)}) collective-permute-start(f32[72,128]{1,0:T(8,128)S(1)} %get-tuple-element.55), channel_id=1, source_target_pairs={{0,2},{1,3},{2,0},{3,1},{4,6},{5,7},{6,4},{7,5},{8,10},{9,11},{10,... | collective-permute-start | bytes 110600 | tf_op jit(solution)/shard_map/ppermute | solution.py:25
  26.7 2.8 %collective-permute-start.11 = (bf16[128,1280]{1,0:T(8,128)(2,1)S(1)}, bf16[128,1280]{1,0:T(8,128)(2,1)S(1)}, u32[]{:S(2)}, u32[]{:S(2)}) collective-permute-start(bf16[128,1280]{1,0:T(8,128)(2,1)S(1)} %pad_maximum_fusion.1.refs_0_), channel_id=1, source_target_pairs={{0,1},{1,0},{2,3},{3,2},{4,5},{5,4},{6,7},{7,6},{8,9},{9,8},{10,11... | collective-permute-start | bytes 983048 | tf_op jit(solution)/shard_map/ppermute | solution.py:25
  26.8 4.0 %collective-permute-start.10 = (f32[72,128]{1,0:T(8,128)S(1)}, f32[72,128]{1,0:T(8,128)S(1)}, u32[]{:S(2)}, u32[]{:S(2)}) collective-permute-start(f32[72,128]{1,0:T(8,128)S(1)} %add_add_fusion), channel_id=1, source_target_pairs={{0,4},{1,5},{2,6},{3,7},{4,0},{5,1},{6,2},{7,3},{8,12},{9,13},{10,... | collective-permute-start | bytes 110600 | tf_op jit(solution)/shard_map/ppermute | solution.py:25
  27.9 9.2 %collective-permute-start.13 = (bf16[64,1280]{1,0:T(8,128)(2,1)S(1)}, bf16[64,1280]{1,0:T(8,128)(2,1)S(1)}, u32[]{:S(2)}, u32[]{:S(2)}) collective-permute-start(bf16[64,1280]{1,0:T(8,128)(2,1)S(1)} %collective-permute-done.5), channel_id=1, source_target_pairs={{0,16},{16,0},{1,17},{17,1},{2,18},{18,2},{3,19},{19,3},{4,20},{20... | collective-permute-start | bytes 491528 | tf_op jit(solution)/shard_map/ppermute | solution.py:206
  31.6 5.5 %collective-permute-start.12 = (bf16[64,1280]{1,0:T(8,128)(2,1)S(1)}, bf16[64,1280]{1,0:T(8,128)(2,1)S(1)}, u32[]{:S(2)}, u32[]{:S(2)}) collective-permute-start(bf16[64,1280]{1,0:T(8,128)(2,1)S(1)} %get-tuple-element.72), channel_id=1, source_target_pairs={{0,2},{1,3},{2,0},{3,1},{4,6},{5,7},{6,4},{7,5},{8,10},{9,11},{10,... | collective-permute-start | bytes 491528 | tf_op jit(solution)/shard_map/ppermute | solution.py:25
  33.1 1.7 %collective-permute-start.19 = (bf16[128,512]{1,0:T(8,128)(2,1)S(1)}, bf16[128,512]{1,0:T(8,128)(2,1)S(1)}, u32[]{:S(2)}, u32[]{:S(2)}) collective-permute-start(bf16[128,512]{1,0:T(8,128)(2,1)S(1)} %slice.42), channel_id=1, source_target_pairs={{0,1},{1,0},{2,3},{3,2},{4,5},{5,4},{6,7},{7,6},{8,9},{9,8},{10,11... | collective-permute-start | bytes 393224 | tf_op jit(solution)/shard_map/ppermute | solution.py:25
  33.2 6.7 %collective-permute-start.18 = (bf16[128,512]{1,0:T(8,128)(2,1)S(1)}, bf16[128,512]{1,0:T(8,128)(2,1)S(1)}, u32[]{:S(2)}, u32[]{:S(2)}) collective-permute-start(bf16[128,512]{1,0:T(8,128)(2,1)S(1)} %slice.35.refs_2_), channel_id=1, source_target_pairs={{0,16},{16,0},{1,17},{17,1},{2,18},{18,2},{3,19},{19,3},{4,20},{20... | collective-permute-start | bytes 393224 | tf_op jit(solution)/shard_map/ppermute | solution.py:206
  34.8 7.2 %collective-permute-start.20 = (bf16[128,512]{1,0:T(8,128)(2,1)S(1)}, bf16[128,512]{1,0:T(8,128)(2,1)S(1)}, u32[]{:S(2)}, u32[]{:S(2)}) collective-permute-start(bf16[128,512]{1,0:T(8,128)(2,1)S(1)} %collective-permute-done.19.refs_3_), channel_id=1, source_target_pairs={{0,16},{16,0},{1,17},{17,1},{2,18},{18,2},{3,19},{19,3},{4,20},{20... | collective-permute-start | bytes 393224 | tf_op jit(solution)/shard_map/ppermute | solution.py:206
  37.2 5.3 %collective-permute-start.17 = (bf16[128,1280]{1,0:T(8,128)(2,1)S(1)}, bf16[128,1280]{1,0:T(8,128)(2,1)S(1)}, u32[]{:S(2)}, u32[]{:S(2)}) collective-permute-start(bf16[128,1280]{1,0:T(8,128)(2,1)S(1)} %constant_dynamic-update-slice_fusion.2.refs_0_), channel_id=1, source_target_pairs={{0,1},{1,0},{2,3},{3,2},{4,5},{5,4},{6,7},{7,6},{8,9},{9,8},{10,11... | collective-permute-start | bytes 983048 | tf_op jit(solution)/shard_map/ppermute | solution.py:25
  37.3 7.0 %collective-permute-start.14 = (bf16[16,1280]{1,0:T(8,128)(2,1)S(1)}, bf16[16,1280]{1,0:T(8,128)(2,1)S(1)}, u32[]{:S(2)}, u32[]{:S(2)}) collective-permute-start(bf16[16,1280]{1,0:T(8,128)(2,1)S(1)} %get-tuple-element.92), channel_id=1, source_target_pairs={{0,12},{1,13},{2,14},{3,15},{4,8},{5,9},{6,10},{7,11},{8,4},{9,5},... | collective-permute-start | bytes 122888 | tf_op jit(solution)/shard_map/ppermute | solution.py:25
  39.7 5.2 %collective-permute-start.15 = (bf16[16,1280]{1,0:T(8,128)(2,1)S(1)}, bf16[16,1280]{1,0:T(8,128)(2,1)S(1)}, u32[]{:S(2)}, u32[]{:S(2)}) collective-permute-start(bf16[16,1280]{1,0:T(8,128)(2,1)S(1)} %get-tuple-element.91), channel_id=1, source_target_pairs={{0,8},{1,9},{2,10},{3,11},{4,12},{5,13},{6,14},{7,15},{8,0},{9,1},... | collective-permute-start | bytes 122888 | tf_op jit(solution)/shard_map/ppermute | solution.py:25
  39.9 5.1 %collective-permute-start.16 = (bf16[16,1280]{1,0:T(8,128)(2,1)S(1)}, bf16[16,1280]{1,0:T(8,128)(2,1)S(1)}, u32[]{:S(2)}, u32[]{:S(2)}) collective-permute-start(bf16[16,1280]{1,0:T(8,128)(2,1)S(1)} %get-tuple-element.90), channel_id=1, source_target_pairs={{0,4},{1,5},{2,6},{3,7},{4,0},{5,1},{6,2},{7,3},{8,12},{9,13},{10,... | collective-permute-start | bytes 122888 | tf_op jit(solution)/shard_map/ppermute | solution.py:25
  45.0 1.3 %collective-permute-start.21 = (f32[8,1280]{1,0:T(8,128)S(1)}, f32[8,1280]{1,0:T(8,128)S(1)}, u32[]{:S(2)}, u32[]{:S(2)}) collective-permute-start(f32[8,1280]{1,0:T(8,128)S(1)} %get-tuple-element.93), channel_id=1, source_target_pairs={{0,1},{1,0},{2,3},{3,2},{4,5},{5,4},{6,7},{7,6},{8,9},{9,8},{10,11... | collective-permute-start | bytes 122888 | tf_op jit(solution)/shard_map/ppermute | solution.py:25
